TPU v7x, 32 devices: a whole 2x2x4 slice. The times are simulated.
32 devices in a mesh: dp: 8 (over z, y), zero: 4 (over x, core).
Axes of the slice: x: 2, y: 2, z: 4, core: 2. Of those that a mesh axis runs over, the one named last changes fastest.
Arguments:
- nodes: float32 [65536, 128], P(('dp', 'zero')), may hold values from -6 to 6
- cotangent: float32 [65536, 128], P(('dp', 'zero')), may hold values from -6 to 6
- lengths: int32 [128], P(('dp', 'zero')), may hold values from 256 to 512, as said below
- w_query: float32 [2, 128, 128], P(None, 'zero'), may hold values from -0.5 to 0.5
- w_key: float32 [2, 128, 128], P(None, 'zero'), may hold values from -0.5 to 0.5
- w_value: float32 [2, 128, 128], P(None, 'zero'), may hold values from -0.5 to 0.5
- w_out: float32 [2, 128, 128], P(None, 'zero'), may hold values from -1 to 1
- b_query: float32 [2, 128], P(None, 'zero'), may hold values from -2 to 2
- b_key: float32 [2, 128], P(None, 'zero'), may hold values from -2 to 2
- b_value: float32 [2, 128], P(None, 'zero'), may hold values from -2 to 2
- b_out: float32 [2, 128], P(None, 'zero'), may hold values from -2 to 2
- gain_key: float32 [2, 128], P(None, 'zero'), may hold values from 0.5 to 1.5
- shift_key: float32 [2, 128], P(None, 'zero'), may hold values from -2 to 2
- gain_value: float32 [2, 128], P(None, 'zero'), may hold values from 0.5 to 1.5
- shift_value: float32 [2, 128], P(None, 'zero'), may hold values from -2 to 2
- w_up: float32 [2, 128, 256], P(None, 'zero'), may hold values from -0.5 to 0.5
- b_up: float32 [2, 256], P(None, 'zero'), may hold values from -2 to 2
- w_down: float32 [2, 256, 128], P(None, 'zero'), may hold values from -0.375 to 0.375
- b_down: float32 [2, 128], P(None, 'zero'), may hold values from -2 to 2
Outputs:
- output: float32 [65536, 128], P(('dp', 'zero'))
- grad_nodes: float32 [65536, 128], P(('dp', 'zero'))
- grad_w_query: float32 [2, 128, 128], P(None, 'zero')
- grad_w_key: float32 [2, 128, 128], P(None, 'zero')
- grad_w_value: float32 [2, 128, 128], P(None, 'zero')
- grad_w_out: float32 [2, 128, 128], P(None, 'zero')
- grad_b_query: float32 [2, 128], P(None, 'zero')
- grad_b_key: float32 [2, 128], P(None, 'zero')
- grad_b_value: float32 [2, 128], P(None, 'zero')
- grad_b_out: float32 [2, 128], P(None, 'zero')
- grad_gain_key: float32 [2, 128], P(None, 'zero')
- grad_shift_key: float32 [2, 128], P(None, 'zero')
- grad_gain_value: float32 [2, 128], P(None, 'zero')
- grad_shift_value: float32 [2, 128], P(None, 'zero')
- grad_w_up: float32 [2, 128, 256], P(None, 'zero')
- grad_b_up: float32 [2, 256], P(None, 'zero')
- grad_w_down: float32 [2, 256, 128], P(None, 'zero')
- grad_b_down: float32 [2, 128], P(None, 'zero')
Inputs may be any that keep to these rules, and one draw needn't show every extreme that they name: Each device's 4 lengths sum to at most 2048, and one of them is exactly 512.
All inputs are finite; a program needn't handle non-finite values.
Results may differ from a plain program's by a relative error of at most 0.0003.
Values sent between devices are 32-bit elements; how exact they have to be, the bound alone decides.
A program may use at most 128 MiB of HBM per device.

v0:
```python
import jax
import jax.numpy as jnp
from jax import lax
from jax.sharding import PartitionSpec as P

HEADS = 4
LAYERS = 2


def product(left, right):
    return jnp.dot(left, right, precision=lax.Precision.HIGHEST)


def segment_tables(lengths, rows):
    ends = jnp.cumsum(lengths)
    starts = ends - lengths
    places = jnp.arange(rows, dtype=jnp.int32)[:, None]
    member = jnp.logical_and(places >= starts[None, :], places < ends[None, :]).astype(jnp.float32)
    live_rows = jnp.sum(member, axis=1, keepdims=True)
    scaled = member / lengths.astype(jnp.float32)[None, :]
    return (member, scaled, live_rows)


def head_norm(values, gain, shift):
    rows = values.shape[0]
    split = values.reshape(rows, HEADS, -1)
    centred = split - jnp.mean(split, axis=2, keepdims=True)
    spread = jnp.mean(centred * centred, axis=2, keepdims=True)
    return (centred * lax.rsqrt(spread + 1e-05)).reshape(rows, -1) * gain + shift


def apply_layer(inputs, params, member, scaled, live_rows):
    (
        w_query,
        w_key,
        w_value,
        w_out,
        b_query,
        b_key,
        b_value,
        b_out,
        gain_key,
        shift_key,
        gain_value,
        shift_value,
        w_up,
        b_up,
        w_down,
        b_down,
    ) = params
    rows = inputs.shape[0]
    query = (product(inputs, w_query) + b_query).reshape(rows, HEADS, -1)
    keys = head_norm(product(inputs, w_key) + b_key, gain_key, shift_key).reshape(rows, HEADS, -1)
    values = head_norm(product(inputs, w_value) + b_value, gain_value, shift_value).reshape(
        rows, HEADS, -1
    )
    summary = jnp.einsum("ts,thk,thv->shkv", scaled, keys, values, precision=lax.Precision.HIGHEST)
    mixed = jnp.einsum(
        "ts,thk,shkv->thv", member, query, summary, precision=lax.Precision.HIGHEST
    ).reshape(rows, -1)
    middle = inputs + live_rows * (product(mixed, w_out) + b_out)
    hidden = jax.nn.gelu(product(middle, w_up) + b_up)
    return middle + live_rows * (product(hidden, w_down) + b_down)


def fetch_forward(shards, level):
    return (
        lax.all_gather(shards[0][level], "zero", axis=0, tiled=True),
        lax.all_gather(shards[1][level], "zero", axis=0, tiled=True),
        lax.all_gather(shards[2][level], "zero", axis=0, tiled=True),
        lax.all_gather(shards[3][level], "zero", axis=0, tiled=True),
        lax.all_gather(shards[4][level], "zero", axis=0, tiled=True),
        lax.all_gather(shards[5][level], "zero", axis=0, tiled=True),
        lax.all_gather(shards[6][level], "zero", axis=0, tiled=True),
        lax.all_gather(shards[7][level], "zero", axis=0, tiled=True),
        lax.all_gather(shards[8][level], "zero", axis=0, tiled=True),
        lax.all_gather(shards[9][level], "zero", axis=0, tiled=True),
        lax.all_gather(shards[10][level], "zero", axis=0, tiled=True),
        lax.all_gather(shards[11][level], "zero", axis=0, tiled=True),
        lax.all_gather(shards[12][level], "zero", axis=0, tiled=True),
        lax.all_gather(shards[13][level], "zero", axis=0, tiled=True),
        lax.all_gather(shards[14][level], "zero", axis=0, tiled=True),
        lax.all_gather(shards[15][level], "zero", axis=0, tiled=True),
    )


def fetch_backward(shards, level):
    return (
        lax.all_gather(shards[0][level], "zero", axis=0, tiled=True),
        lax.all_gather(shards[1][level], "zero", axis=0, tiled=True),
        lax.all_gather(shards[2][level], "zero", axis=0, tiled=True),
        lax.all_gather(shards[3][level], "zero", axis=0, tiled=True),
        lax.all_gather(shards[4][level], "zero", axis=0, tiled=True),
        lax.all_gather(shards[5][level], "zero", axis=0, tiled=True),
        lax.all_gather(shards[6][level], "zero", axis=0, tiled=True),
        lax.all_gather(shards[7][level], "zero", axis=0, tiled=True),
        lax.all_gather(shards[8][level], "zero", axis=0, tiled=True),
        lax.all_gather(shards[9][level], "zero", axis=0, tiled=True),
        lax.all_gather(shards[10][level], "zero", axis=0, tiled=True),
        lax.all_gather(shards[11][level], "zero", axis=0, tiled=True),
        lax.all_gather(shards[12][level], "zero", axis=0, tiled=True),
        lax.all_gather(shards[13][level], "zero", axis=0, tiled=True),
        lax.all_gather(shards[14][level], "zero", axis=0, tiled=True),
        lax.all_gather(shards[15][level], "zero", axis=0, tiled=True),
    )


def reduce_grads(grads):
    shares = (
        lax.psum_scatter(grads[0], "zero", scatter_dimension=0, tiled=True),
        lax.psum_scatter(grads[1], "zero", scatter_dimension=0, tiled=True),
        lax.psum_scatter(grads[2], "zero", scatter_dimension=0, tiled=True),
        lax.psum_scatter(grads[3], "zero", scatter_dimension=0, tiled=True),
        lax.psum_scatter(grads[4], "zero", scatter_dimension=0, tiled=True),
        lax.psum_scatter(grads[5], "zero", scatter_dimension=0, tiled=True),
        lax.psum_scatter(grads[6], "zero", scatter_dimension=0, tiled=True),
        lax.psum_scatter(grads[7], "zero", scatter_dimension=0, tiled=True),
        lax.psum_scatter(grads[8], "zero", scatter_dimension=0, tiled=True),
        lax.psum_scatter(grads[9], "zero", scatter_dimension=0, tiled=True),
        lax.psum_scatter(grads[10], "zero", scatter_dimension=0, tiled=True),
        lax.psum_scatter(grads[11], "zero", scatter_dimension=0, tiled=True),
        lax.psum_scatter(grads[12], "zero", scatter_dimension=0, tiled=True),
        lax.psum_scatter(grads[13], "zero", scatter_dimension=0, tiled=True),
        lax.psum_scatter(grads[14], "zero", scatter_dimension=0, tiled=True),
        lax.psum_scatter(grads[15], "zero", scatter_dimension=0, tiled=True),
    )
    return lax.psum(
        (
            shares[0],
            shares[1],
            shares[2],
            shares[3],
            shares[4],
            shares[5],
            shares[6],
            shares[7],
            shares[8],
            shares[9],
            shares[10],
            shares[11],
            shares[12],
            shares[13],
            shares[14],
            shares[15],
        ),
        "dp",
    )


def local(
    nodes,
    cotangent,
    lengths,
    w_query,
    w_key,
    w_value,
    w_out,
    b_query,
    b_key,
    b_value,
    b_out,
    gain_key,
    shift_key,
    gain_value,
    shift_value,
    w_up,
    b_up,
    w_down,
    b_down,
):
    shards = (
        w_query,
        w_key,
        w_value,
        w_out,
        b_query,
        b_key,
        b_value,
        b_out,
        gain_key,
        shift_key,
        gain_value,
        shift_value,
        w_up,
        b_up,
        w_down,
        b_down,
    )
    member, scaled, live_rows = segment_tables(lengths, nodes.shape[0])
    state = nodes
    kept_inputs = []
    kept_weights = []
    for level in range(LAYERS):
        gathered = fetch_forward(shards, level)
        kept_inputs.append(state)
        kept_weights.append(gathered)
        state = apply_layer(state, gathered, member, scaled, live_rows)
    incoming = cotangent
    reduced = [None] * LAYERS
    for level in reversed(range(LAYERS)):
        weights_now = fetch_backward(shards, level)
        _, pull = jax.vjp(
            lambda a, w: apply_layer(a, w, member, scaled, live_rows),
            kept_inputs[level],
            weights_now,
        )
        incoming, grad_weights = pull(incoming)
        reduced[level] = reduce_grads(grad_weights)
    stacked = tuple(
        (jnp.stack([reduced[level][which] for level in range(LAYERS)]) for which in range(16))
    )
    return (state, incoming) + stacked


def solution(mesh):
    in_specs = (
        P(("dp", "zero"), None),
        P(("dp", "zero"), None),
        P(("dp", "zero")),
        P(None, "zero", None),
        P(None, "zero", None),
        P(None, "zero", None),
        P(None, "zero", None),
        P(None, "zero"),
        P(None, "zero"),
        P(None, "zero"),
        P(None, "zero"),
        P(None, "zero"),
        P(None, "zero"),
        P(None, "zero"),
        P(None, "zero"),
        P(None, "zero", None),
        P(None, "zero"),
        P(None, "zero", None),
        P(None, "zero"),
    )
    out_specs = (
        P(("dp", "zero"), None),
        P(("dp", "zero"), None),
        P(None, "zero", None),
        P(None, "zero", None),
        P(None, "zero", None),
        P(None, "zero", None),
        P(None, "zero"),
        P(None, "zero"),
        P(None, "zero"),
        P(None, "zero"),
        P(None, "zero"),
        P(None, "zero"),
        P(None, "zero"),
        P(None, "zero"),
        P(None, "zero", None),
        P(None, "zero"),
        P(None, "zero", None),
        P(None, "zero"),
    )
    return jax.shard_map(local, mesh=mesh, in_specs=in_specs, out_specs=out_specs, check_vma=False)
```

profile of v0, /device:TPU:0, one launch (start us, length us, event | category | flops | bytes accessed | tf_op | source)
XLA Modules:
  0.0 563.6 jit_solution(8801854964088064192)
XLA Ops:
  26.0 13.3 %all-reduce.42 = (f32[128]{0:T(128)S(1)}, f32[128]{0:T(128)S(1)}, f32[128]{0:T(128)S(1)}, f32[128]{0:T(128)S(1)}, f32[128]{0:T(128)S(1)}, /*index=5*/f32[128]{0:...) all-reduce(f32[128]{0:T(128)S(1)} %bitcast_dynamic-update-slice_fus, ...), channel_id=9, replica_groups=mesh['dp'=8,'zero'=4] {'zero'}, use_global_device_ids=true, to_apply=%add.4 | all-reduce | flops 2688 | bytes 21504
  42.5 5.2 all-gather.26
  47.8 5.2 all-gather.22
  53.0 5.2 all-gather.18
  58.2 5.2 all-gather.16
  63.5 5.2 all-gather.10
  68.7 5.2 all-gather.6
  73.9 5.2 all-gather.2
  79.2 5.2 all-gather
  86.0 5.4 all-gather.30
  91.4 5.4 all-gather.28
  96.8 5.4 all-gather.14
  102.2 5.6 all-gather.12
  203.1 5.4 fusion.12
  235.3 6.7 %fusion.67 = f32[256,128]{1,0:T(8,128)} fusion(f32[2048,256]{1,0:T(8,128)} %copy-done.52, f32[2048,128]{1,0:T(8,128)} %param.20, f32[2048]{0:T(1024)S(1)} %get-tuple-element.150), kind=kOutput, calls=%fused_computation.136 | convolution fusion | flops 809762816 | bytes 3284992 | tf_op jit(solution)/shard_map/transpose(jvp())/dot_general | solution.py:11
  251.0 6.7 %fusion.66 = f32[256,128]{1,0:T(8,128)} fusion(f32[2048,256]{1,0:T(8,128)} %copy-done.53, f32[2048,128]{1,0:T(8,128)} %copy-done.46, f32[2048]{0:T(1024)S(1)} %get-tuple-element.150), kind=kOutput, calls=%fused_computation.135 | convolution fusion | flops 809762816 | bytes 3284992 | tf_op jit(solution)/shard_map/transpose(jvp())/dot_general | solution.py:11
  270.3 10.7 %all-reduce.41 = (f32[128]{0:T(128)S(1)}, f32[128]{0:T(128)S(1)}, f32[128]{0:T(128)S(1)}, f32[128]{0:T(128)S(1)}, f32[128]{0:T(128)S(1)}, /*index=5*/f32[128]{0:...) all-reduce(f32[128]{0:T(128)S(1)} %bitcast_dynamic-update-slice_fus, ...), channel_id=33, replica_groups=mesh['dp'=8,'zero'=4] {'zero'}, use_global_device_ids=true, to_apply=%add.19 | all-reduce | flops 2944 | bytes 23552
  308.2 5.7 %reduce-scatter.27.cloned.1.call-done = f32[32,128]{1,0:T(8,128)} async-done(((f32[128,128]{1,0:T(8,128)}), f32[32,128]{1,0:T(8,128)}) %reduce-scatter.27.cloned.1.call-update) | async-done | bytes 16400 | tf_op jit(solution)/shard_map/reduce_scatter | solution.py:113
  313.9 22.0 %reduce-scatter.25.cloned.1.call-done = f32[32,128]{1,0:T(8,128)} async-done(((f32[128,128]{1,0:T(8,128)}), f32[32,128]{1,0:T(8,128)}) %reduce-scatter.25.cloned.1.call-update) | async-done | bytes 16400 | tf_op jit(solution)/shard_map/reduce_scatter | solution.py:113
  335.9 22.0 %reduce-scatter.35.cloned.1.call-done = f32[64,128]{1,0:T(8,128)} async-done(((f32[256,128]{1,0:T(8,128)}), f32[64,128]{1,0:T(8,128)}) %reduce-scatter.35.cloned.1.call-update) | async-done | bytes 32784 | tf_op jit(solution)/shard_map/reduce_scatter | solution.py:124
  358.0 22.0 %reduce-scatter.31.cloned.1.call-done = f32[32,256]{1,0:T(8,128)} async-done(((f32[128,256]{1,0:T(8,128)}), f32[32,256]{1,0:T(8,128)}) %reduce-scatter.31.cloned.1.call-update) | async-done | bytes 32784 | tf_op jit(solution)/shard_map/reduce_scatter | solution.py:122
  380.0 22.0 %reduce-scatter.29.cloned.1.call-done = f32[32,256]{1,0:T(8,128)} async-done(((f32[128,256]{1,0:T(8,128)}), f32[32,256]{1,0:T(8,128)}) %reduce-scatter.29.cloned.1.call-update) | async-done | bytes 32784 | tf_op jit(solution)/shard_map/reduce_scatter | solution.py:122
  402.0 22.0 %reduce-scatter.33.cloned.1.call-done = f32[64,128]{1,0:T(8,128)} async-done(((f32[256,128]{1,0:T(8,128)}), f32[64,128]{1,0:T(8,128)}) %reduce-scatter.33.cloned.1.call-update) | async-done | bytes 32784 | tf_op jit(solution)/shard_map/reduce_scatter | solution.py:124
  426.9 106.4 %all-reduce.45.cloned.1.call-done = (f32[1,32,128]{1,2,0:T(8,128)}, f32[1,32,128]{1,2,0:T(8,128)}, f32[1,32,128]{1,2,0:T(8,128)}, f32[1,32,128]{1,2,0:T(8,128)},...) async-done(((f32[1,32,128]{1,2,0:T(8,128)}, ...) | async-done | bytes 264976 | tf_op jit(solution)/shard_map/psum | solution.py:127
  (472 shorter events, 216.3 us)
Async XLA Ops:
  7.2 100.6 %copy-start = (f32[2048,128]{1,0:T(8,128)S(1)}, f32[2048,128]{1,0:T(8,128)}, u32[]{:S(2)}) copy-start(f32[2048,128]{1,0:T(8,128)} %param.19) | copy-start | bytes 3145732
  7.2 292.4 %reduce-scatter.43.cloned.1.call-start = ((), (), s32[]{:S(2)}) async-start(), calls=%async_computation.21 | async-start | bytes 81920
  39.3 72.5 %copy-start.101 = (f32[128]{0:T(128)}, f32[128]{0:T(128)S(1)}, u32[]{:S(2)}) copy-start(f32[128]{0:T(128)S(1)} %get-tuple-element.124) | copy-start | bytes 1540
  39.3 72.9 %copy-start.102 = (f32[128]{0:T(128)}, f32[128]{0:T(128)S(1)}, u32[]{:S(2)}) copy-start(f32[128]{0:T(128)S(1)} %get-tuple-element.121) | copy-start | bytes 1540
  39.3 90.2 %copy-start.104 = (f32[128]{0:T(128)}, f32[128]{0:T(128)S(1)}, u32[]{:S(2)}) copy-start(f32[128]{0:T(128)S(1)} %get-tuple-element.131) | copy-start | bytes 1540
  42.4 153.6 %copy-start.70 = (f32[2048,4]{0,1:T(4,128)}, f32[2048,4]{0,1:T(4,128)S(1)}, u32[]{:S(2)}) copy-start(f32[2048,4]{0,1:T(4,128)S(1)} %fusion.117) | copy-start | bytes 98308
  42.5 120.3 %copy-start.69 = (f32[2048,4]{0,1:T(4,128)}, f32[2048,4]{0,1:T(4,128)S(1)}, u32[]{:S(2)}) copy-start(f32[2048,4]{0,1:T(4,128)S(1)} %get-tuple-element.151) | copy-start | bytes 98308
  53.0 72.4 %copy-start.81 = (f32[1,128,128]{2,1,0:T(8,128)}, f32[1,128,128]{2,1,0:T(8,128)S(1)}, u32[]{:S(2)}) copy-start(f32[1,128,128]{2,1,0:T(8,128)S(1)} %all-gather.22) | copy-start | bytes 196612
  58.2 68.6 %copy-start.83 = (f32[1,128,128]{2,1,0:T(8,128)}, f32[1,128,128]{2,1,0:T(8,128)S(1)}, u32[]{:S(2)}) copy-start(f32[1,128,128]{2,1,0:T(8,128)S(1)} %all-gather.18) | copy-start | bytes 196612
  63.5 64.9 %copy-start.79 = (f32[1,128,128]{2,1,0:T(8,128)}, f32[1,128,128]{2,1,0:T(8,128)S(1)}, u32[]{:S(2)}) copy-start(f32[1,128,128]{2,1,0:T(8,128)S(1)} %all-gather.16) | copy-start | bytes 196612
  68.7 50.1 %copy-start.77 = (f32[1,128,128]{2,1,0:T(8,128)}, f32[1,128,128]{2,1,0:T(8,128)S(1)}, u32[]{:S(2)}) copy-start(f32[1,128,128]{2,1,0:T(8,128)S(1)} %all-gather.10) | copy-start | bytes 196612
  162.1 138.9 %reduce-scatter.47.cloned.1.call-start = ((), (), s32[]{:S(2)}) async-start(), calls=%async_computation.23 | async-start | bytes 81920
  172.2 130.3 %reduce-scatter.39.cloned.1.call-start = ((), (), s32[]{:S(2)}) async-start(), calls=%async_computation.19 | async-start | bytes 81920
  181.0 122.9 %reduce-scatter.37.cloned.1.call-start = ((), (), s32[]{:S(2)}) async-start(), calls=%async_computation.18 | async-start | bytes 81920
  202.8 102.6 %reduce-scatter.45.cloned.1.call-start = ((), (), s32[]{:S(2)}) async-start(), calls=%async_computation.22 | async-start | bytes 81920
  217.8 89.0 %reduce-scatter.41.cloned.1.call-start = ((), (), s32[]{:S(2)}) async-start(), calls=%async_computation.20 | async-start | bytes 81920
  228.0 85.9 %reduce-scatter.27.cloned.1.call-start = ((), (), s32[]{:S(2)}) async-start(), calls=%async_computation.13 | async-start | bytes 81920 | tf_op jit(solution)/shard_map/reduce_scatter | solution.py:113
  232.0 103.9 %reduce-scatter.25.cloned.1.call-start = ((), (), s32[]{:S(2)}) async-start(), calls=%async_computation.12 | async-start | bytes 81920 | tf_op jit(solution)/shard_map/reduce_scatter | solution.py:113
  235.2 122.7 %reduce-scatter.35.cloned.1.call-start = ((), (), s32[]{:S(2)}) async-start(), calls=%async_computation.17 | async-start | bytes 163840 | tf_op jit(solution)/shard_map/reduce_scatter | solution.py:124
  242.1 137.9 %reduce-scatter.31.cloned.1.call-start = ((), (), s32[]{:S(2)}) async-start(), calls=%async_computation.15 | async-start | bytes 163840 | tf_op jit(solution)/shard_map/reduce_scatter | solution.py:122
  246.2 155.8 %reduce-scatter.29.cloned.1.call-start = ((), (), s32[]{:S(2)}) async-start(), calls=%async_computation.14 | async-start | bytes 163840 | tf_op jit(solution)/shard_map/reduce_scatter | solution.py:122
  250.7 173.3 %reduce-scatter.33.cloned.1.call-start = ((), (), s32[]{:S(2)}) async-start(), calls=%async_computation.16 | async-start | bytes 163840 | tf_op jit(solution)/shard_map/reduce_scatter | solution.py:124
  257.7 275.6 %all-reduce.45.cloned.1.call-start = ((), (), s32[]{:S(2)}) async-start(), calls=%async_computation.24 | async-start | bytes 1134592 | tf_op jit(solution)/shard_map/psum | solution.py:127
  297.8 126.3 %copy-start.72 = (f32[1,128,128]{2,1,0:T(8,128)S(1)}, f32[1,128,128]{2,1,0:T(8,128)}, u32[]{:S(2)}) copy-start(f32[1,128,128]{2,1,0:T(8,128)} %copy-done.71) | copy-start | bytes 196612
  (107 other events, 650.2 us)
Sparse Core Ops, SparseCore 0:
  162.2 19.7 reduce-scatter.42
  184.6 19.4 reduce-scatter.46
  206.5 19.3 reduce-scatter.38
  228.9 19.4 reduce-scatter.36
  250.7 19.4 reduce-scatter.44
  272.5 19.4 reduce-scatter.40
  294.4 19.4 reduce-scatter.26
  316.4 19.4 reduce-scatter.24
  338.4 19.5 reduce-scatter.34
  360.4 19.5 reduce-scatter.30
  382.4 19.5 reduce-scatter.28
  404.4 19.5 reduce-scatter.32
  432.2 101.0 all-reduce.44
where the time goes:
time: 571 us; the launch traced here: 564 us
  waiting for transfers between devices  222 us (39%)
  matrix products  139 us (24%)
  blocking collectives  87.7 us (15%)
  local copies, waits for them, and re-layouts  62.2 us (11%)
  other arithmetic  31.8 us (6%)
  between operations  18.6 us (3%)
    psum x1, waiting for transfers between devices, reduce_grads(): lax.psum((shares[0], shares[1], shares[2], shares[3], shares[4], shares[5...  106 us
    dot_general x33, matrix products, product(): return jnp.dot(left, right, precision=lax.Precision.HIGHEST)  83.6 us
    reduce_scatter x2, waiting for transfers between devices, reduce_grads(): lax.psum_scatter(grads[14], 'zero', scatter_dimension=0, tiled=True)  44.1 us
    reduce_scatter x2, waiting for transfers between devices, reduce_grads(): lax.psum_scatter(grads[12], 'zero', scatter_dimension=0, tiled=True)  44.1 us
    unnamed x286, local copies, waits for them, and re-layouts  37.9 us
    reduce_scatter x2, waiting for transfers between devices, reduce_grads(): lax.psum_scatter(grads[3], 'zero', scatter_dimension=0, tiled=True)  27.7 us
    dot_general x6, matrix products, apply_layer(): jnp.einsum('ts,thk,thv->shkv', scaled, keys, values, precision=lax.Precis...  25.2 us
    unnamed x2, blocking collectives  24 us
  transfers between devices with their start and end apart: 13, of which 7 were waited for; matrix products, arithmetic and copies ran while one was open for 23% of the time, Pallas kernels for 0%

commit v1 on v0

v1 whole, which is shorter than its diff:
```python
import jax
import jax.numpy as jnp
from jax import lax
from jax.experimental import pallas as pl
from jax.experimental.pallas import tpu as pltpu
from jax.sharding import PartitionSpec as P

D=128; FF=256; SEGS=4; BLK=512; TOK=2048; HD=32
F32=jnp.float32; BF=jnp.bfloat16
VM=pltpu.VMEM

def split(x):
    hi=x.astype(BF); lo=(x-hi.astype(F32)).astype(BF)
    return hi,lo
def pack(x):
    return jnp.concatenate(split(x),axis=1)
def quad(x):
    p=pack(x)
    return jnp.concatenate([p,p],axis=0)
def mm(a,b):
    return jnp.dot(a,b,preferred_element_type=F32)
def tn(a,b):
    return lax.dot_general(a,b,(((0,),(0,)),((),())),preferred_element_type=F32)
def halves(r):
    n=r.shape[1]//2
    return r[:,:n]+r[:,n:]
def quads(r):
    m=r.shape[0]//2
    return halves(r[:m]+r[m:])
def prod(a,b):
    return halves(mm(pack(a),quad(b)))
def part(x):
    return jnp.sum(x.reshape(x.shape[0]//8,8,x.shape[1]),axis=0)

def group_mask():
    r=lax.broadcasted_iota(jnp.int32,(D,D),0)//HD
    c=lax.broadcasted_iota(jnp.int32,(D,D),1)//HD
    return r==c

BQ,BK,BV,BO,GK,SK,GV,SV,BD,BU0,BU1=range(11)

LAYER_SCRATCH=dict(
    X=((TOK,2*D),BF), H=((TOK,D),F32), NK=((TOK,D),F32), NV=((TOK,D),F32), RK=((TOK,D),F32), RV=((TOK,D),F32),
    KN=((TOK,2*D),BF), VN=((TOK,2*D),BF), MD=((TOK,2*D),BF), ACT=((TOK,2*FF),BF), DG=((TOK,FF),F32),
    WKV=((2*D,4*D),BF), WUP=((2*D,2*FF),BF), WDN=((2*FF,2*D),BF), WDNT=((2*D,2*FF),BF), WUPT=((2*FF,2*D),BF),
    WKVT=((4*D,2*D),BF), WO2=((2*D,2*D),BF), WOT2=((2*D,2*D),BF), WQL=((D,2*D),BF), WQTL=((D,2*D),BF),
    S=((SEGS,D,D),F32), T=((SEGS,D,D),F32), UT2=((SEGS,2*D,2*D),BF), U2=((SEGS,2*D,2*D),BF), UB=((SEGS,8,D),F32),
    CB=((8,D),F32),
)
TMP_SCRATCH=dict(
    E=((TOK,D),F32), ED=((TOK,2*D),BF), EP=((TOK,2*FF),BF), EM=((TOK,D),F32), EO=((TOK,2*D),BF), FKV=((TOK,4*D),BF),
    A2=((2*D,D),BF),
)

def prep_kv(L,w,vec,A2):
    a1=A2[0:D,:]
    b=vec[BK:BV+1,:]
    b8=jnp.concatenate([b,jnp.zeros((6,D),F32)],axis=0)
    L['CB'][...]=center(b8,a1)
    wk=center(w['k'][...],a1); wv=center(w['v'][...],a1)
    kh,kl=split(wk); vh,vl=split(wv)
    kv=jnp.concatenate([kh,vh,kl,vl],axis=1)
    L['WKV'][0:D,:]=kv; L['WKV'][D:,:]=kv
    L['WKVT'][0:2*D,:]=quad(wk.T); L['WKVT'][2*D:,:]=quad(wv.T)

def prep_qo(L,w):
    wo=w['o'][...]
    L['WO2'][...]=quad(wo); L['WOT2'][...]=quad(wo.T)
    wq=w['q'][...]
    L['WQL'][...]=pack(wq); L['WQTL'][...]=pack(wq.T)

def prep_ff(L,w):
    L['WUP'][...]=quad(w['up'][...])
    L['WDN'][...]=quad(w['dn'][...])

def prep_back(L,w):
    L['WUPT'][...]=quad(w['up'][...].T)
    L['WDNT'][...]=quad(w['dn'][...].T)

def fwd_a(L,vec,A2,live,r0,n):
    rows=pl.ds(r0,n)
    x=pack(L['H'][rows,:])
    L['X'][rows,:]=x
    r=mm(x,L['WKV'][...])
    a2=A2[...]
    lv=live(r0,n)
    for i,(N,R,O,g,s) in enumerate((('NK','RK','KN',GK,SK),('NV','RV','VN',GV,SV))):
        c=r[:,i*D:(i+1)*D]+r[:,(i+2)*D:(i+3)*D]+L['CB'][i:i+1,:]
        rs=lax.rsqrt(mm(pack(c*c),a2)+1e-5)
        nn=c*rs
        L[R][rows,:]=rs; L[N][rows,:]=nn
        y=jnp.where(lv,nn*vec[g:g+1,:]+vec[s:s+1,:],0.0)
        L[O][rows,:]=pack(y)

def fwd_s(L,vec,gm,s,inv):
    rows=pl.ds(s*BLK,BLK)
    S=jnp.where(gm,quads(tn(L['KN'][rows,:],L['VN'][rows,:]))*inv,0.0)
    L['S'][s]=S
    t=halves(mm(pack(S),L['WO2'][...]))
    L['T'][s]=t
    t2=quad(t)
    u=halves(mm(L['WQL'][...],t2))
    bq=jnp.broadcast_to(vec[BQ:BQ+1,:],(8,D))
    L['UB'][s]=halves(mm(pack(bq),t2))+vec[BO:BO+1,:]
    L['U2'][s]=quad(u)
    L['UT2'][s]=quad(u.T)

def fwd_c(L,vec,OUT,s,r0,n):
    rows=pl.ds(r0,n)
    mid=L['H'][rows,:]+halves(mm(L['X'][rows,:],L['U2'][s]))+L['UB'][s,0:1,:]
    md=pack(mid); L['MD'][rows,:]=md
    bu=jnp.concatenate([vec[BU0:BU0+1,:],vec[BU1:BU1+1,:]],axis=1)
    z=halves(mm(md,L['WUP'][...]))+bu
    z2=z*z
    c0=0.7978845608028654
    t=jnp.tanh(z*(c0+(c0*0.044715)*z2))
    p=0.5*t+0.5
    act=z*p
    L['DG'][rows,:]=p+act*(1.0-p)*((2*c0)+(6*c0*0.044715)*z2)
    act2=pack(act)
    L['ACT'][rows,:]=act2
    OUT[rows,:]=mid+halves(mm(act2,L['WDN'][...]))+vec[BD:BD+1,:]

def bwd_a(L,Tm,r0,n):
    rows=pl.ds(r0,n)
    e=Tm['E'][rows,:]
    ed=pack(e); Tm['ED'][rows,:]=ed
    ep=halves(mm(ed,L['WDNT'][...]))*L['DG'][rows,:]
    ep2=pack(ep); Tm['EP'][rows,:]=ep2
    em=e+halves(mm(ep2,L['WUPT'][...]))
    Tm['EM'][rows,:]=em
    Tm['EO'][rows,:]=pack(em)
    return part(e),part(ep),part(em)

def bwd_s(L,vec,Tm,gm,s,inv,c):
    rows=pl.ds(s*BLK,BLK)
    H=quads(tn(L['X'][rows,:],Tm['EO'][rows,:]))
    c1=jnp.sum(c,axis=0,keepdims=True)
    H2=quad(H)
    P=halves(mm(L['WQTL'][...],H2))+vec[BQ:BQ+1,:].T*c1
    es=jnp.where(gm,halves(mm(pack(P),L['WOT2'][...]))*inv,0.0)
    t2=quad(L['T'][s].T)
    gq=halves(mm(pack(H),t2))
    gbq=halves(mm(pack(c),t2))
    go=halves(mm(pack(L['S'][s].T),quad(P)))
    return quad(es.T),quad(es),gq,gbq,go

def bwd_b(L,vec,Tm,A2,esT2,es2,r0,n):
    rows=pl.ds(r0,n)
    a2=A2[...]
    out=[]
    for i,(N,R,O,g,w) in enumerate((('NK','RK','VN',GK,esT2),('NV','RV','KN',GV,es2))):
        en=halves(mm(L[O][rows,:],w))
        nn=L[N][rows,:]
        m=en*vec[g:g+1,:]
        mn=m*nn
        av=mm(pack(mn),a2)
        f=L[R][rows,:]*(m-nn*av)
        Tm['FKV'][rows,i*2*D:(i+1)*2*D]=pack(f)
        out+= [part(en),part(en*nn),part(f)]
    return out

def bwd_x(L,Tm,DX,s,r0,n):
    rows=pl.ds(r0,n)
    DX[rows,:]=Tm['EM'][rows,:]+halves(mm(Tm['FKV'][rows,:],L['WKVT'][...])+mm(Tm['EO'][rows,:],L['UT2'][s]))


MESH = pl.DeviceIdType.MESH
NAMES = ("k", "v", "q", "o", "up", "dn")
ARG = dict(q=0, k=1, v=2, o=3, up=12, dn=14)
VECS = ((4, BQ), (5, BK), (6, BV), (7, BO), (8, GK), (9, SK), (10, GV), (11, SV), (15, BD), (13, BU0))
SMALL = 16
GROUPS = (
    ((1, "up"), (1, "dn"), (1, "q"), (1, "o"), (1, "k"), (1, "v"), (1, "small")),
    ((0, "up"), (0, "dn"), (0, "q"), (0, "o")),
    ((0, "k"), (0, "v"), (0, "small")),
)


def shard(name, n_zero):
    if name == "dn":
        return FF // n_zero, D
    return D // n_zero, FF if name == "up" else D


def group_layout(n_dp, n_zero):
    places, sizes, pieces = {}, [], []
    for g, members in enumerate(GROUPS):
        at = 0
        for item in members:
            places[item] = (g, at)
            if item[1] == "small":
                at += SMALL
            else:
                rows, cols = shard(item[1], n_zero)
                at += rows * cols // D
        sizes.append(at)
        pieces.append(-(-at // (8 * n_dp)) * 8)
    return places, sizes, pieces


def center(x, a1):
    h = x.astype(BF)
    r = x - h.astype(F32)
    m = r.astype(BF)
    lo = (r - m.astype(F32)).astype(BF)
    return x - (mm(h, a1) + mm(m, a1) + mm(lo, a1))


def one(x):
    return jnp.sum(x, axis=0, keepdims=True)


class Names:
    pass


def fused_kernel(n_dp, n_zero, order, *refs):
    R = Names()
    for name, ref in zip(order, refs):
        setattr(R, name, ref)
    places, sizes, pieces = group_layout(n_dp, n_zero)
    dp, zero = lax.axis_index("dp"), lax.axis_index("zero")
    zpeer = [None] + [lax.rem(zero + k, n_zero) for k in range(1, n_zero)]
    zfrom = [None] + [lax.rem(zero + n_zero - k, n_zero) for k in range(1, n_zero)]
    dpeer = [None] + [lax.rem(dp + k, n_dp) for k in range(1, n_dp)]
    dfrom = [None] + [lax.rem(dp + n_dp - k, n_dp) for k in range(1, n_dp)]

    barrier = pltpu.get_barrier_semaphore()
    for k in range(1, n_zero):
        pl.semaphore_signal(barrier, inc=1, device_id=(dp, zpeer[k]), device_id_type=MESH)
    for k in range(1, n_dp):
        pl.semaphore_signal(barrier, inc=1, device_id=(dpeer[k], zero), device_id_type=MESH)

    small_in = []
    for i, (arg, _) in enumerate(VECS):
        c = pltpu.make_async_copy(R.params[arg], R.stage[i], R.stage_sem.at[i])
        c.start()
        small_in.append(c)
    nodes_in = pltpu.make_async_copy(R.nodes, R.nodes_v, R.io_sem.at[0])
    nodes_in.start()

    def rows_of(name, who):
        n = shard(name, n_zero)[0]
        return pl.ds(pl.multiple_of(who * n, n), n)

    own = {}
    for level in range(2):
        for i, name in enumerate(NAMES):
            own[level, name] = pltpu.make_async_copy(
                R.params[ARG[name]].at[level],
                R.weights[name].at[level, rows_of(name, zero), :],
                R.own_sem.at[level, i],
            )
    for level in range(2):
        for name in NAMES:
            own[level, name].start()
    cot_in = pltpu.make_async_copy(R.cotangent, R.cot_v, R.io_sem.at[1])
    cot_in.start()

    pl.semaphore_wait(barrier, n_zero - 1 + n_dp - 1)

    def weight_copy(level, name, k, who):
        i = NAMES.index(name)
        return pltpu.make_async_remote_copy(
            src_ref=R.params[ARG[name]].at[level],
            dst_ref=R.weights[name].at[level, rows_of(name, who), :],
            send_sem=R.w_send.at[level, i, k - 1],
            recv_sem=R.w_recv.at[level, i, k - 1],
            device_id=(dp, zpeer[k]),
            device_id_type=MESH,
        )

    def send_weights(level, names):
        for name in names:
            for k in range(1, n_zero):
                weight_copy(level, name, k, zero).start()

    def take_weights(level, names):
        for name in names:
            own[level, name].wait()
            for k in range(1, n_zero):
                weight_copy(level, name, k, zfrom[k]).wait_recv()

    send_weights(0, ("k", "v"))

    for c in small_in:
        c.wait()
    lane = lax.broadcasted_iota(jnp.int32, (2, D), 1)
    R.vec_own[...] = jnp.zeros((2, SMALL, D), F32)
    for i, (arg, row) in enumerate(VECS):
        x = R.stage[i][...]
        n = x.shape[1]
        x = jnp.concatenate([x, jnp.zeros((2, D - n), F32)], axis=1)
        x = pltpu.roll(x, lax.rem(zero * n, D), axis=1)
        if row != BU0:
            R.vec_own[:, row, :] = x
        else:
            first = zero * n < D
            R.vec_own[:, row, :] = jnp.where(first, x, 0.0)
            R.vec_own[:, row + 1, :] = jnp.where(first, 0.0, x)

    def vec_copy(k):
        return pltpu.make_async_remote_copy(
            src_ref=R.vec_own,
            dst_ref=R.vec_in.at[k - 1],
            send_sem=R.vec_send.at[k - 1],
            recv_sem=R.vec_recv.at[k - 1],
            device_id=(dp, zpeer[k]),
            device_id_type=MESH,
        )

    for k in range(1, n_zero):
        vec_copy(k).start()
    send_weights(0, ("q", "o", "up", "dn"))
    send_weights(1, NAMES)

    gm = group_mask()
    a = jnp.where(gm, 1.0 / HD, 0.0).astype(BF)
    R.A2[0:D, :] = a
    R.A2[D:, :] = a
    ln = [R.lengths[i] for i in range(SEGS)]
    st = [0]
    for i in range(SEGS):
        st.append(st[-1] + ln[i])
    inv = [1.0 / (jnp.full((1, D), ln[s], jnp.int32).astype(F32)) for s in range(SEGS)]

    def live(r0, n):
        s = r0 // BLK
        return lax.broadcasted_iota(jnp.int32, (n, D), 0) + (r0 - s * BLK) < ln[s]

    Ls, Tm = R.layers, R.temps
    Tm["A2"] = R.A2
    nodes_in.wait()
    for s in range(SEGS):
        Ls[0]["H"][s * BLK : (s + 1) * BLK, :] = R.nodes_v[pl.ds(st[s], BLK), :]

    for k in range(1, n_zero):
        vec_copy(k).wait_recv()
    vecs = []
    for level in range(2):
        x = R.vec_own[level]
        for k in range(1, n_zero):
            x = x + R.vec_in[k - 1, level]
        R.vec[level] = x
        vecs.append(R.vec.at[level])

    for level in range(2):
        L = Ls[level]
        dst = Ls[1]["H"] if level == 0 else R.Y
        w = {n: R.weights[n].at[level] for n in NAMES}
        take_weights(level, ("k", "v"))
        prep_kv(L, w, vecs[level], R.A2)
        for s in range(SEGS):
            fwd_a(L, vecs[level], R.A2, live, s * BLK, BLK)
        take_weights(level, ("q", "o"))
        prep_qo(L, w)
        for s in range(SEGS):
            fwd_s(L, vecs[level], gm, s, inv[s])
        take_weights(level, ("up", "dn"))
        prep_ff(L, w)
        for s in range(SEGS):
            fwd_c(L, vecs[level], dst, s, s * BLK, BLK)

    cot_in.wait()
    for s in range(SEGS):
        x = R.cot_v[pl.ds(st[s], BLK), :]
        Tm["E"][s * BLK : (s + 1) * BLK, :] = jnp.where(live(s * BLK, BLK), x, 0.0)

    def put(level, name, g):
        grp, at = places[level, name]
        n = shard(name, n_zero)[0]
        for p in range(n_zero):
            part_p = g[p * n : (p + 1) * n]
            if name == "up":
                R.gsend[grp][p, at : at + n, :] = part_p[:, :D]
                R.gsend[grp][p, at + n : at + 2 * n, :] = part_p[:, D:]
            else:
                R.gsend[grp][p, at : at + n, :] = part_p

    def zero_copy(grp, k):
        return pltpu.make_async_remote_copy(
            src_ref=R.gsend[grp].at[zpeer[k]],
            dst_ref=R.gzero[grp].at[k - 1],
            send_sem=R.z_send.at[grp, k - 1],
            recv_sem=R.z_recv.at[grp, k - 1],
            device_id=(dp, zpeer[k]),
            device_id_type=MESH,
        )

    def start_zero(grp):
        for k in range(1, n_zero):
            zero_copy(grp, k).start()

    def piece_copy(grp, k):
        return pltpu.make_async_remote_copy(
            src_ref=R.gred[grp].at[dpeer[k]],
            dst_ref=R.gdp[grp].at[k - 1],
            send_sem=R.d_send.at[grp, k - 1],
            recv_sem=R.d_recv.at[grp, k - 1],
            device_id=(dpeer[k], zero),
            device_id_type=MESH,
        )

    def final_copy(grp, k, who):
        return pltpu.make_async_remote_copy(
            src_ref=R.gfin[grp].at[dp],
            dst_ref=R.gfin[grp].at[who],
            send_sem=R.f_send.at[grp, k - 1],
            recv_sem=R.f_recv.at[grp, k - 1],
            device_id=(dpeer[k], zero),
            device_id_type=MESH,
        )

    def start_dp(grp):
        for k in range(1, n_zero):
            zero_copy(grp, k).wait_recv()
        total, piece = sizes[grp], pieces[grp]
        for j in range(n_dp):
            lo, hi = j * piece, min((j + 1) * piece, total)
            if lo < hi:
                x = R.gsend[grp][zero, lo:hi, :]
                for k in range(1, n_zero):
                    x = x + R.gzero[grp][k - 1, lo:hi, :]
                R.gred[grp][j, 0 : hi - lo, :] = x
            if hi - lo < piece:
                lo = max(hi - lo, 0)
                R.gred[grp][j, lo:piece, :] = jnp.zeros((piece - lo, D), F32)
        for k in range(1, n_dp):
            piece_copy(grp, k).start()

    def start_final(grp):
        x = R.gred[grp][dp]
        for k in range(1, n_dp):
            piece_copy(grp, k).wait_recv()
            x = x + R.gdp[grp][k - 1]
        R.gfin[grp][dp] = x
        for k in range(1, n_dp):
            final_copy(grp, k, dp).start()

    def end_final(grp):
        for k in range(1, n_dp):
            final_copy(grp, k, dfrom[k]).wait_recv()
        c = pltpu.make_async_copy(R.gfin[grp], R.fin_out[grp], R.io_sem.at[4 + grp])
        c.start()
        return c

    shift = [jnp.minimum(BLK * s - st[s], (BLK - 256) * s) for s in range(SEGS)]

    def unpack(o, base):
        lo, hi = (0, 256, 512, 768), (512, 1024, 1536, 2048)
        step = 256
        for t0 in range(0, TOK, step):
            it = lax.broadcasted_iota(jnp.int32, (step, D), 0) + t0
            x = base[t0 : t0 + step, :]
            for s in range(SEGS):
                if t0 < hi[s] and t0 + step > lo[s]:
                    y = R.Y[pl.ds(t0 + shift[s], step), :]
                    x = jnp.where((it >= st[s]) & (it < st[s + 1]), y, x)
            o[t0 : t0 + step, :] = x

    R.Y[TOK:, :] = jnp.zeros((R.Y.shape[0] - TOK, D), F32)
    unpack(R.nodes_v, R.nodes_v)
    store_out = pltpu.make_async_copy(R.nodes_v, R.out, R.io_sem.at[2])
    store_out.start()

    zero8 = jnp.zeros((8, D), F32)
    for level in (1, 0):
        L = Ls[level]
        w = {n: R.weights[n].at[level] for n in NAMES}
        prep_back(L, w)
        sb, su, sc = zero8, jnp.zeros((8, FF), F32), []
        for s in range(SEGS):
            b, u, o = bwd_a(L, Tm, s * BLK, BLK)
            sb, su = sb + b, su + u
            sc.append(o)
        if level == 0:
            start_dp(0)
        put(level, "dn", quads(tn(L["ACT"][...], Tm["ED"][...])))
        put(level, "up", quads(tn(L["MD"][...], Tm["EP"][...])))
        gq = go = jnp.zeros((D, D), F32)
        gbq = zero8
        es = []
        for s in range(SEGS):
            eT, e2, q1, b1, o1 = bwd_s(L, vecs[level], Tm, gm, s, inv[s], sc[s])
            gq, go, gbq = gq + q1, go + o1, gbq + b1
            es.append((eT, e2))
        put(level, "q", gq)
        put(level, "o", go)
        if level == 0:
            start_zero(1)
        ss = [zero8] * 6
        for s in range(SEGS):
            o = bwd_b(L, vecs[level], Tm, R.A2, *es[s], s * BLK, BLK)
            ss = [x + y for x, y in zip(ss, o)]
        a1 = R.A2[0:D, :]
        gkv = tn(L["X"][...], Tm["FKV"][...])
        gkv = gkv[0:D] + gkv[D:]
        put(level, "k", center(halves(gkv[:, : 2 * D]), a1))
        put(level, "v", center(halves(gkv[:, 2 * D :]), a1))
        rows = [None] * SMALL
        rows[BQ], rows[BK], rows[BV] = one(gbq), one(center(ss[2], a1)), one(center(ss[5], a1))
        rows[BO] = one(sc[0] + sc[1] + sc[2] + sc[3])
        rows[SK], rows[GK], rows[SV], rows[GV] = one(ss[0]), one(ss[1]), one(ss[3]), one(ss[4])
        rows[BD] = one(sb)
        u = one(su)
        rows[BU0], rows[BU1] = u[:, :D], u[:, D:]
        rows = [jnp.zeros((1, D), F32) if r is None else r for r in rows]
        small = jnp.concatenate(rows, axis=0)
        grp, at = places[level, "small"]
        for p in range(n_zero):
            R.gsend[grp][p, at : at + SMALL, :] = small
        start_zero(0 if level == 1 else 2)
        if level == 0:
            start_final(0)
        dst = Tm["E"] if level == 1 else R.Y
        for s in range(SEGS):
            bwd_x(L, Tm, dst, s, s * BLK, BLK)

    start_dp(1)
    start_dp(2)
    unpack(R.cot_v, R.cot_v)
    store_gx = pltpu.make_async_copy(R.cot_v, R.gx, R.io_sem.at[3])
    store_gx.start()
    start_final(1)
    start_final(2)
    last = [store_out, store_gx] + [end_final(g) for g in range(3)]

    for level in range(2):
        for name in NAMES:
            for k in range(1, n_zero):
                weight_copy(level, name, k, zero).wait_send()
    for k in range(1, n_zero):
        vec_copy(k).wait_send()
    for g in range(3):
        for k in range(1, n_zero):
            zero_copy(g, k).wait_send()
        for k in range(1, n_dp):
            piece_copy(g, k).wait_send()
            final_copy(g, k, dp).wait_send()
    for c in last:
        c.wait()


def finish_kernel(n_dp, n_zero, order, *refs):
    R = Names()
    for name, ref in zip(order, refs):
        setattr(R, name, ref)
    places, sizes, pieces = group_layout(n_dp, n_zero)
    copies = []

    def copy(src, dst):
        c = pltpu.make_async_copy(src, dst, R.sem.at[len(copies)])
        c.start()
        copies.append(c)

    fins = []
    for g in range(3):
        c = pltpu.make_async_copy(R.fin[g], R.fin_v[g], R.fin_sem.at[g])
        c.start()
        fins.append(c)
    half = TOK // 2
    for i in range(2):
        copy(R.out.at[pl.ds(i * half, half), :], R.outs[0].at[pl.ds(i * half, half), :])
        copy(R.gx.at[pl.ds(i * half, half), :], R.outs[1].at[pl.ds(i * half, half), :])
    for c in fins:
        c.wait()
    for name, arg in ARG.items():
        for level in range(2):
            g, at = places[level, name]
            n = shard(name, n_zero)[0]
            if name == "up":
                for h in range(2):
                    copy(
                        R.fin_v[g].at[pl.ds(at + h * n, n), :],
                        R.outs[2 + arg].at[level, :, pl.ds(h * D, D)],
                    )
            else:
                copy(R.fin_v[g].at[pl.ds(at, n), :], R.outs[2 + arg].at[level])
    zero = lax.axis_index("zero")
    small = []
    for level in range(2):
        g, at = places[level, "small"]
        small.append(R.fin_v[g][at : at + SMALL, :])
    for arg, row in VECS:
        n = R.outs[2 + arg].shape[1]
        x = jnp.concatenate([s[row : row + 1, :] for s in small], axis=0)
        if row == BU0:
            x1 = jnp.concatenate([s[row + 1 : row + 2, :] for s in small], axis=0)
            x = jnp.where(zero * n < D, x, x1)
        x = pltpu.roll(x, lax.rem(D - lax.rem(zero * n, D), D), axis=1)
        R.outs[2 + arg][...] = x[:, :n]
    for c in copies:
        c.wait()


def make_fused(n_dp, n_zero, params):
    places, sizes, pieces = group_layout(n_dp, n_zero)
    dma = pltpu.SemaphoreType.DMA
    any_ = pl.BlockSpec(memory_space=pl.ANY)
    order, scratch = [], []

    def add(name, shape):
        order.append(name)
        scratch.append(shape)

    def sds(*shape):
        return jax.ShapeDtypeStruct(shape, F32)

    n_params = len(params)
    out_shape = [sds(TOK, D), sds(TOK, D)] + [sds(n_dp, p, D) for p in pieces]
    ls, ts = list(LAYER_SCRATCH), [n for n in TMP_SCRATCH if n != "A2"]
    for level in range(2):
        for n in ls:
            add(("layer", level, n), VM(*LAYER_SCRATCH[n]))
    for n in ts:
        add(("temp", n), VM(*TMP_SCRATCH[n]))
    add("A2", VM(*TMP_SCRATCH["A2"]))
    add("Y", VM((TOK + 768, D), F32))
    add("nodes_v", VM((TOK, D), F32))
    add("cot_v", VM((TOK, D), F32))
    for i, (arg, _) in enumerate(VECS):
        add(("stage", i), VM(params[arg].shape, F32))
    for n in NAMES:
        rows, cols = shard(n, n_zero)
        add(("weights", n), VM((2, rows * n_zero, cols), F32))
    add("vec_own", VM((2, SMALL, D), F32))
    add("vec_in", VM((n_zero - 1, 2, SMALL, D), F32))
    add("vec", VM((2, SMALL, D), F32))
    for g in range(3):
        add(("gsend", g), VM((n_zero, sizes[g], D), F32))
        add(("gzero", g), VM((n_zero - 1, sizes[g], D), F32))
        add(("gred", g), VM((n_dp, pieces[g], D), F32))
        add(("gdp", g), VM((n_dp - 1, pieces[g], D), F32))
        add(("gfin", g), VM((n_dp, pieces[g], D), F32))
    add("stage_sem", dma((len(VECS),)))
    add("io_sem", dma((8,)))
    add("own_sem", dma((2, 6)))
    add("w_send", dma((2, 6, n_zero - 1)))
    add("w_recv", dma((2, 6, n_zero - 1)))
    add("vec_send", dma((n_zero - 1,)))
    add("vec_recv", dma((n_zero - 1,)))
    for n, m in (("z", n_zero), ("d", n_dp), ("f", n_dp)):
        add(n + "_send", dma((3, m - 1)))
        add(n + "_recv", dma((3, m - 1)))

    def body(*refs):
        lengths, nodes, cot = refs[:3]
        pr = refs[3 : 3 + n_params]
        outs = refs[3 + n_params : 8 + n_params]
        rest = refs[8 + n_params :]
        simple = dict(lengths=lengths, nodes=nodes, cotangent=cot, params=pr, out=outs[0], gx=outs[1], fin_out=outs[2:5])
        layers, temps = [{}, {}], {}
        simple.update(layers=layers, temps=temps, stage=[None] * len(VECS), weights={})
        for n in ("gsend", "gzero", "gred", "gdp", "gfin"):
            simple[n] = [None] * 3
        for key, ref in zip(order, rest):
            if isinstance(key, str):
                simple[key] = ref
            elif key[0] == "layer":
                layers[key[1]][key[2]] = ref
            elif key[0] == "temp":
                temps[key[1]] = ref
            else:
                simple[key[0]][key[1]] = ref
        fused_kernel(n_dp, n_zero, list(simple), *simple.values())

    call = pl.pallas_call(
        body,
        out_shape=out_shape,
        in_specs=[pl.BlockSpec(memory_space=pltpu.SMEM)] + [any_] * (2 + n_params),
        out_specs=[any_] * 5,
        scratch_shapes=scratch,
        compiler_params=pltpu.CompilerParams(
            collective_id=0, has_side_effects=True, vmem_limit_bytes=60 * 1024 * 1024
        ),
    )
    return call


def make_finish(n_dp, n_zero, params):
    places, sizes, pieces = group_layout(n_dp, n_zero)
    any_ = pl.BlockSpec(memory_space=pltpu.HBM)
    vmem = pl.BlockSpec(memory_space=pltpu.VMEM)
    out_shape = [jax.ShapeDtypeStruct((TOK, D), F32)] * 2
    out_shape += [jax.ShapeDtypeStruct(p.shape, F32) for p in params]
    weights = set(ARG.values())
    out_specs = [any_] * 2 + [any_ if i in weights else vmem for i in range(len(params))]

    def body(*refs):
        out, gx = refs[:2]
        fin = refs[2:5]
        outs = refs[5 : 7 + len(params)]
        rest = refs[7 + len(params) :]
        simple = dict(out=out, gx=gx, fin=fin, outs=outs, fin_v=rest[:3], sem=rest[3], fin_sem=rest[4])
        finish_kernel(n_dp, n_zero, list(simple), *simple.values())

    return pl.pallas_call(
        body,
        out_shape=out_shape,
        in_specs=[any_] * 5,
        out_specs=out_specs,
        scratch_shapes=[VM((n_dp * p, D), F32) for p in pieces]
        + [pltpu.SemaphoreType.DMA((18,)), pltpu.SemaphoreType.DMA((3,))],
        compiler_params=pltpu.CompilerParams(vmem_limit_bytes=32 * 1024 * 1024),
    )


def solution(mesh):
    n_dp, n_zero = mesh.shape["dp"], mesh.shape["zero"]
    wide, flat = P(None, "zero", None), P(None, "zero")
    params = (wide,) * 4 + (flat,) * 8 + (wide, flat, wide, flat)
    rows = P(("dp", "zero"), None)

    def local(nodes, cotangent, lengths, *params):
        out, gx, *fins = make_fused(n_dp, n_zero, params)(lengths, nodes, cotangent, *params)
        fins = [f.reshape(-1, D) for f in fins]
        return tuple(make_finish(n_dp, n_zero, params)(out, gx, *fins))

    return jax.shard_map(
        local,
        mesh=mesh,
        in_specs=(rows, rows, P(("dp", "zero"))) + params,
        out_specs=(rows, rows) + params,
        check_vma=False,
    )
```

time: 571 us -> 70.8 us (0.12); the launches traced: 564 us -> 70.5 us
  waiting for transfers between devices: 222 us -> 0 us
  matrix products: 139 us -> 0 us
  blocking collectives: 87.7 us -> 0 us
  Pallas kernels: 0 us -> 64.6 us
  local copies, waits for them, and re-layouts: 62.2 us -> 5.09 us
  other arithmetic: 31.8 us -> 0 us
  between operations: 18.6 us -> 0.85 us
    dot_general x45 -> x0, matrix products: 132 us -> none  [the longest x33 83.6 us: product(): return jnp.dot(left, right, precision=lax.Precision.HIGHEST)]
    reduce_scatter x6 -> x0, waiting for transfers between devices: 116 us -> none  [the longest x2 44.1 us: reduce_grads(): lax.psum_scatter(grads[14], 'zero', scatter_dimension=0, tiled=True)]
    psum x1 -> x0, waiting for transfers between devices: 106 us -> none  [reduce_grads(): lax.psum((shares[0], shares[1], shares[2], shares[3], shares[4], shares[5...]
    pallas_call x0 -> x2, Pallas kernels: none -> 64.6 us  [the longest x1 61.9 us: local(): make_fused(n_dp, n_zero, params)(lengths, nodes, cotangent, *params)]
    all_gather x12 -> x0, blocking collectives: 63.7 us -> none  [the longest x2 11 us: fetch_forward(): lax.all_gather(shards[12][level], 'zero', axis=0, tiled=True)]
    unnamed x286 -> x10, local copies, waits for them, and re-layouts: 37.9 us -> 5.09 us
    unnamed x2 -> x0, blocking collectives: 24 us -> none
    another operation x17 -> x0, other arithmetic: 18.9 us -> none  [the longest x16 18.1 us: local(): jnp.stack([reduced[level][which] for level in range(LAYERS)])]
  transfers between devices with their start and end apart: 13 -> 0, of which waited for: 7 -> 0; matrix products, arithmetic and copies ran while one was open for 23% -> 0% of each run, Pallas kernels for 0% -> 0%
where the time goes in v1:
time: 70.8 us; the launch traced here: 70.5 us
  Pallas kernels  64.6 us (91%)
  local copies, waits for them, and re-layouts  5.09 us (7%)
  between operations  0.85 us (1%)
    pallas_call x1, Pallas kernels, local(): make_fused(n_dp, n_zero, params)(lengths, nodes, cotangent, *params)  61.9 us
    unnamed x10, local copies, waits for them, and re-layouts  5.09 us
    pallas_call x1, Pallas kernels, local(): return tuple(make_finish(n_dp, n_zero, params)(out, gx, *fins))  2.65 us

profile of v1, /device:TPU:0, one launch (start us, length us, event | category | flops | bytes accessed | tf_op | source)
XLA Modules:
  0.0 70.5 jit_solution(17246161762585699892)
XLA Ops:
  0.7 61.9 %shard_map.322 = (f32[2048,128]{1,0:T(8,128)}, f32[2048,128]{1,0:T(8,128)}, f32[8,40,128]{2,1,0:T(8,128)}, f32[8,24,128]{2,1,0:T(8,128)}, f32[8,16,128]{2,1,0:T(8,128)}) custom-call(s32[4]{0:T(128)} %refs_0_.1, f32[2048,128]{1,0:T(8,128)} %refs_1_.1, f32[2048,128]{1,0:T(8,128)} %refs_2_.1, f32[2,32,128]{2,1,0:T(8,128)} %refs_3_.1, f32[2,32,128]{2,1,0:T(8,128)} %refs_4_.1, ...), custom_call_target="tpu_custom_call" | custom-call | tf_op jit(solution)/shard_map/pallas_call | solution.py:716
  62.6 0.0 copy-start
  62.6 1.2 %copy-done = f32[2048,128]{1,0:T(8,128)S(1)} copy-done((f32[2048,128]{1,0:T(8,128)S(1)}, f32[2048,128]{1,0:T(8,128)}, u32[]{:S(2)}) %copy-start) | copy-done | bytes 1048600
  63.8 0.0 copy-start.1
  63.8 1.2 %copy-done.1 = f32[2048,128]{1,0:T(8,128)S(1)} copy-done((f32[2048,128]{1,0:T(8,128)S(1)}, f32[2048,128]{1,0:T(8,128)}, u32[]{:S(2)}) %copy-start.1) | copy-done | bytes 1048600
  65.1 0.0 copy-start.2
  65.1 0.9 %copy-done.2 = f32[8,40,128]{2,1,0:T(8,128)S(1)} copy-done((f32[8,40,128]{2,1,0:T(8,128)S(1)}, f32[8,40,128]{2,1,0:T(8,128)}, u32[]{:S(2)}) %copy-start.2) | copy-done | bytes 163864
  66.0 0.0 copy-start.3
  66.0 0.9 %copy-done.3 = f32[8,24,128]{2,1,0:T(8,128)S(1)} copy-done((f32[8,24,128]{2,1,0:T(8,128)S(1)}, f32[8,24,128]{2,1,0:T(8,128)}, u32[]{:S(2)}) %copy-start.3) | copy-done | bytes 98328
  66.9 0.0 copy-start.4
  66.9 0.8 %copy-done.4 = f32[8,16,128]{2,1,0:T(8,128)S(1)} copy-done((f32[8,16,128]{2,1,0:T(8,128)S(1)}, f32[8,16,128]{2,1,0:T(8,128)}, u32[]{:S(2)}) %copy-start.4) | copy-done | bytes 65560
  67.7 2.6 %shard_map.323 = (f32[2048,128]{1,0:T(8,128)}, f32[2048,128]{1,0:T(8,128)}, f32[2,32,128]{2,1,0:T(8,128)}, f32[2,32,128]{2,1,0:T(8,128)}, f32[2,32,128]{2,1,0:T(...) custom-call(f32[2048,128]{1,0:T(8,128)S(1)} %copy-done, ...), custom_call_target="tpu_custom_call" | custom-call | tf_op jit(solution)/shard_map/pallas_call | solution.py:718
Async XLA Ops:
  62.6 1.2 %copy-start = (f32[2048,128]{1,0:T(8,128)S(1)}, f32[2048,128]{1,0:T(8,128)}, u32[]{:S(2)}) copy-start(f32[2048,128]{1,0:T(8,128)} %get-tuple-element.23.refs_0_) | copy-start | bytes 3145732
  63.8 1.2 %copy-start.1 = (f32[2048,128]{1,0:T(8,128)S(1)}, f32[2048,128]{1,0:T(8,128)}, u32[]{:S(2)}) copy-start(f32[2048,128]{1,0:T(8,128)} %get-tuple-element.24.refs_1_) | copy-start | bytes 3145732
  65.1 0.9 %copy-start.2 = (f32[8,40,128]{2,1,0:T(8,128)S(1)}, f32[8,40,128]{2,1,0:T(8,128)}, u32[]{:S(2)}) copy-start(f32[8,40,128]{2,1,0:T(8,128)} %get-tuple-element.25) | copy-start | bytes 491524
  66.0 0.9 %copy-start.3 = (f32[8,24,128]{2,1,0:T(8,128)S(1)}, f32[8,24,128]{2,1,0:T(8,128)}, u32[]{:S(2)}) copy-start(f32[8,24,128]{2,1,0:T(8,128)} %get-tuple-element.26) | copy-start | bytes 294916
  66.9 0.8 %copy-start.4 = (f32[8,16,128]{2,1,0:T(8,128)S(1)}, f32[8,16,128]{2,1,0:T(8,128)}, u32[]{:S(2)}) copy-start(f32[8,16,128]{2,1,0:T(8,128)} %get-tuple-element.27) | copy-start | bytes 196612

commit v2 on v1

--- a/solution.py
+++ b/solution.py
@@ -12,39 +12,49 @@
 def split(x):
     hi=x.astype(BF); lo=(x-hi.astype(F32)).astype(BF)
     return hi,lo
+def cat0(*x): return jnp.concatenate(x,axis=0)
+def cat1(*x): return jnp.concatenate(x,axis=1)
 def pack(x):
-    return jnp.concatenate(split(x),axis=1)
+    return cat1(*split(x))
 def quad(x):
     p=pack(x)
-    return jnp.concatenate([p,p],axis=0)
+    return cat0(p,p)
+def quad_t(x):
+    h,l=split(x)
+    return cat0(cat1(h,h),cat1(l,l))
 def mm(a,b):
     return jnp.dot(a,b,preferred_element_type=F32)
 def tn(a,b):
     return lax.dot_general(a,b,(((0,),(0,)),((),())),preferred_element_type=F32)
+def nt(a,b):
+    return lax.dot_general(a,b,(((1,),(1,)),((),())),preferred_element_type=F32)
 def halves(r):
     n=r.shape[1]//2
     return r[:,:n]+r[:,n:]
 def quads(r):
     m=r.shape[0]//2
     return halves(r[:m]+r[m:])
-def prod(a,b):
-    return halves(mm(pack(a),quad(b)))
 def part(x):
     return jnp.sum(x.reshape(x.shape[0]//8,8,x.shape[1]),axis=0)
-
+def one(x):
+    return jnp.sum(x,axis=0,keepdims=True)
 def group_mask():
     r=lax.broadcasted_iota(jnp.int32,(D,D),0)//HD
     c=lax.broadcasted_iota(jnp.int32,(D,D),1)//HD
     return r==c
+def center(x,a1):
+    h=x.astype(BF); r=x-h.astype(F32); m=r.astype(BF); lo=(r-m.astype(F32)).astype(BF)
+    return x-(mm(h,a1)+mm(m,a1)+mm(lo,a1))
 
 BQ,BK,BV,BO,GK,SK,GV,SV,BD,BU0,BU1=range(11)
+AUG=D+16
 
 LAYER_SCRATCH=dict(
     X=((TOK,2*D),BF), H=((TOK,D),F32), NK=((TOK,D),F32), NV=((TOK,D),F32), RK=((TOK,D),F32), RV=((TOK,D),F32),
     KN=((TOK,2*D),BF), VN=((TOK,2*D),BF), MD=((TOK,2*D),BF), ACT=((TOK,2*FF),BF), DG=((TOK,FF),F32),
-    WKV=((2*D,4*D),BF), WUP=((2*D,2*FF),BF), WDN=((2*FF,2*D),BF), WDNT=((2*D,2*FF),BF), WUPT=((2*FF,2*D),BF),
-    WKVT=((4*D,2*D),BF), WO2=((2*D,2*D),BF), WOT2=((2*D,2*D),BF), WQL=((D,2*D),BF), WQTL=((D,2*D),BF),
-    S=((SEGS,D,D),F32), T=((SEGS,D,D),F32), UT2=((SEGS,2*D,2*D),BF), U2=((SEGS,2*D,2*D),BF), UB=((SEGS,8,D),F32),
+    WKV=((2*D,4*D),BF), WUP=((2*D,2*FF),BF), WDN=((2*FF,2*D),BF), WDNT=((2*FF,2*D),BF), WUPT=((2*D,2*FF),BF),
+    WKVT=((2*D,4*D),BF), WO2=((2*D,2*D),BF), WOT2=((2*D,2*D),BF), WQA=((AUG,2*D),BF),
+    SP=((SEGS*D,2*D),BF), TP=((2*D,SEGS*D),BF), UT2=((SEGS,2*D,2*D),BF), U2=((SEGS,2*D,2*D),BF), UB=((SEGS,8,D),F32),
     CB=((8,D),F32),
 )
 TMP_SCRATCH=dict(
@@ -54,33 +64,37 @@
 
 def prep_kv(L,w,vec,A2):
     a1=A2[0:D,:]
-    b=vec[BK:BV+1,:]
-    b8=jnp.concatenate([b,jnp.zeros((6,D),F32)],axis=0)
+    b8=cat0(vec[BK:BV+1,:],jnp.zeros((6,D),F32))
     L['CB'][...]=center(b8,a1)
     wk=center(w['k'][...],a1); wv=center(w['v'][...],a1)
     kh,kl=split(wk); vh,vl=split(wv)
-    kv=jnp.concatenate([kh,vh,kl,vl],axis=1)
+    kv=cat1(kh,vh,kl,vl)
     L['WKV'][0:D,:]=kv; L['WKV'][D:,:]=kv
-    L['WKVT'][0:2*D,:]=quad(wk.T); L['WKVT'][2*D:,:]=quad(wv.T)
-
-def prep_qo(L,w):
+    L['WKVT'][0:D,:]=cat1(kh,kh,vh,vh); L['WKVT'][D:,:]=cat1(kl,kl,vl,vl)
+
+def prep_qo(L,w,vec):
     wo=w['o'][...]
-    L['WO2'][...]=quad(wo); L['WOT2'][...]=quad(wo.T)
-    wq=w['q'][...]
-    L['WQL'][...]=pack(wq); L['WQTL'][...]=pack(wq.T)
+    L['WO2'][...]=quad(wo); L['WOT2'][...]=quad_t(wo)
+    L['WQA'][0:D,:]=pack(w['q'][...])
+    L['WQA'][D:,:]=pack(cat0(vec[BQ:BQ+1,:],jnp.zeros((15,D),F32)))
 
 def prep_ff(L,w):
-    L['WUP'][...]=quad(w['up'][...])
-    L['WDN'][...]=quad(w['dn'][...])
+    up=w['up'][...]
+    L['WUP'][...]=quad(up)
+    dn=w['dn'][...]
+    L['WDN'][...]=quad(dn)
 
 def prep_back(L,w):
-    L['WUPT'][...]=quad(w['up'][...].T)
-    L['WDNT'][...]=quad(w['dn'][...].T)
-
-def fwd_a(L,vec,A2,live,r0,n):
+    L['WUPT'][...]=quad_t(w['up'][...])
+    L['WDNT'][...]=quad_t(w['dn'][...])
+
+def fwd_a(L,vec,A2,live,r0,n,fresh):
     rows=pl.ds(r0,n)
-    x=pack(L['H'][rows,:])
-    L['X'][rows,:]=x
+    if fresh:
+        x=pack(L['H'][rows,:])
+        L['X'][rows,:]=x
+    else:
+        x=L['X'][rows,:]
     r=mm(x,L['WKV'][...])
     a2=A2[...]
     lv=live(r0,n)
@@ -92,65 +106,102 @@
         y=jnp.where(lv,nn*vec[g:g+1,:]+vec[s:s+1,:],0.0)
         L[O][rows,:]=pack(y)
 
-def fwd_s(L,vec,gm,s,inv):
-    rows=pl.ds(s*BLK,BLK)
-    S=jnp.where(gm,quads(tn(L['KN'][rows,:],L['VN'][rows,:]))*inv,0.0)
-    L['S'][s]=S
-    t=halves(mm(pack(S),L['WO2'][...]))
-    L['T'][s]=t
-    t2=quad(t)
-    u=halves(mm(L['WQL'][...],t2))
-    bq=jnp.broadcast_to(vec[BQ:BQ+1,:],(8,D))
-    L['UB'][s]=halves(mm(pack(bq),t2))+vec[BO:BO+1,:]
-    L['U2'][s]=quad(u)
-    L['UT2'][s]=quad(u.T)
-
-def fwd_c(L,vec,OUT,s,r0,n):
+def fwd_s(L,vec,gm,inv):
+    for s in range(SEGS):
+        rows=pl.ds(s*BLK,BLK)
+        S=jnp.where(gm,quads(tn(L['KN'][rows,:],L['VN'][rows,:]))*inv[s],0.0)
+        L['SP'][s*D:(s+1)*D,:]=pack(S)
+    T=halves(mm(L['SP'][...],L['WO2'][...]))
+    ts=[T[s*D:(s+1)*D] for s in range(SEGS)]
+    sp=[split(t) for t in ts]
+    for s in range(SEGS):
+        L['TP'][0:D,s*D:(s+1)*D]=sp[s][0]; L['TP'][D:,s*D:(s+1)*D]=sp[s][1]
+    row=cat1(*[x for hl in sp for x in hl])
+    u=mm(L['WQA'][...],cat0(row,row))
+    for s in range(SEGS):
+        us=halves(u[:,s*2*D:(s+1)*2*D])
+        L['UB'][s]=us[D:D+8]+vec[BO:BO+1,:]
+        h,l=split(us[:D])
+        p=cat1(h,l)
+        L['U2'][s,0:D,:]=p; L['U2'][s,D:,:]=p
+        L['UT2'][s,0:D,:]=cat1(h,h); L['UT2'][s,D:,:]=cat1(l,l)
+
+def fwd_c1(L,s,r0,n):
     rows=pl.ds(r0,n)
     mid=L['H'][rows,:]+halves(mm(L['X'][rows,:],L['U2'][s]))+L['UB'][s,0:1,:]
-    md=pack(mid); L['MD'][rows,:]=md
-    bu=jnp.concatenate([vec[BU0:BU0+1,:],vec[BU1:BU1+1,:]],axis=1)
-    z=halves(mm(md,L['WUP'][...]))+bu
+    L['MD'][rows,:]=pack(mid)
+    return mid
+
+def fwd_c2(L,vec,r0,n):
+    rows=pl.ds(r0,n)
+    bu=cat1(vec[BU0:BU0+1,:],vec[BU1:BU1+1,:])
+    z=halves(mm(L['MD'][rows,:],L['WUP'][...]))+bu
     z2=z*z
     c0=0.7978845608028654
     t=jnp.tanh(z*(c0+(c0*0.044715)*z2))
     p=0.5*t+0.5
     act=z*p
     L['DG'][rows,:]=p+act*(1.0-p)*((2*c0)+(6*c0*0.044715)*z2)
-    act2=pack(act)
-    L['ACT'][rows,:]=act2
-    OUT[rows,:]=mid+halves(mm(act2,L['WDN'][...]))+vec[BD:BD+1,:]
-
-def bwd_a(L,Tm,r0,n):
+    L['ACT'][rows,:]=pack(act)
+
+def fwd_c3(L,vec,OUT,mid,r0,n):
     rows=pl.ds(r0,n)
-    e=Tm['E'][rows,:]
-    ed=pack(e); Tm['ED'][rows,:]=ed
-    ep=halves(mm(ed,L['WDNT'][...]))*L['DG'][rows,:]
-    ep2=pack(ep); Tm['EP'][rows,:]=ep2
-    em=e+halves(mm(ep2,L['WUPT'][...]))
+    OUT[rows,:]=mid+halves(mm(L['ACT'][rows,:],L['WDN'][...]))+vec[BD:BD+1,:]
+
+def bwd_a1(L,Tm,r0,n,fresh):
+    rows=pl.ds(r0,n)
+    if fresh:
+        e=Tm['E'][rows,:]
+        ed=pack(e); Tm['ED'][rows,:]=ed
+        se=part(e)
+    else:
+        ed=Tm['ED'][rows,:]; se=None
+    ep=halves(nt(ed,L['WDNT'][...]))*L['DG'][rows,:]
+    Tm['EP'][rows,:]=pack(ep)
+    return se,part(ep)
+
+def bwd_a2(L,Tm,r0,n):
+    rows=pl.ds(r0,n)
+    em=Tm['E'][rows,:]+halves(nt(Tm['EP'][rows,:],L['WUPT'][...]))
     Tm['EM'][rows,:]=em
     Tm['EO'][rows,:]=pack(em)
-    return part(e),part(ep),part(em)
-
-def bwd_s(L,vec,Tm,gm,s,inv,c):
-    rows=pl.ds(s*BLK,BLK)
-    H=quads(tn(L['X'][rows,:],Tm['EO'][rows,:]))
-    c1=jnp.sum(c,axis=0,keepdims=True)
-    H2=quad(H)
-    P=halves(mm(L['WQTL'][...],H2))+vec[BQ:BQ+1,:].T*c1
-    es=jnp.where(gm,halves(mm(pack(P),L['WOT2'][...]))*inv,0.0)
-    t2=quad(L['T'][s].T)
-    gq=halves(mm(pack(H),t2))
-    gbq=halves(mm(pack(c),t2))
-    go=halves(mm(pack(L['S'][s].T),quad(P)))
-    return quad(es.T),quad(es),gq,gbq,go
+    return part(em)
+
+def bwd_s1(L,Tm,c):
+    hs=[]
+    for s in range(SEGS):
+        rows=pl.ds(s*BLK,BLK)
+        H=quads(tn(L['X'][rows,:],Tm['EO'][rows,:]))
+        hs.append(split(cat0(H,one(c[s]),jnp.zeros((15,D),F32))))
+    return hs
+
+def bwd_s2(L,hs):
+    P=tn(L['WQA'][...],cat1(*[x for hl in hs for x in hl]))
+    P=P[:D]+P[D:]
+    pp=cat0(*[pack(halves(P[:,s*2*D:(s+1)*2*D])) for s in range(SEGS)])
+    return pp
+
+def bwd_s3(L,gm,inv,pp):
+    es=halves(nt(pp,L['WOT2'][...]))
+    out=[]
+    for s in range(SEGS):
+        e=jnp.where(gm,es[s*D:(s+1)*D]*inv[s],0.0)
+        h,l=split(e); p=cat1(h,l)
+        out.append((cat0(cat1(h,h),cat1(l,l)),cat0(p,p)))
+    return out
+
+def bwd_s4(L,hs,pp):
+    go=quads(tn(L['SP'][...],pp))
+    gq=halves(nt(cat0(cat1(*[h for h,l in hs]),cat1(*[l for h,l in hs])),L['TP'][...]))
+    gq=gq[:AUG]+gq[AUG:]
+    return gq[:D],gq[D:D+1],go
 
 def bwd_b(L,vec,Tm,A2,esT2,es2,r0,n):
     rows=pl.ds(r0,n)
     a2=A2[...]
     out=[]
-    for i,(N,R,O,g,w) in enumerate((('NK','RK','VN',GK,esT2),('NV','RV','KN',GV,es2))):
-        en=halves(mm(L[O][rows,:],w))
+    for i,(N,R,O,g,f,w) in enumerate((('NK','RK','VN',GK,nt,esT2),('NV','RV','KN',GV,mm,es2))):
+        en=halves(f(L[O][rows,:],w))
         nn=L[N][rows,:]
         m=en*vec[g:g+1,:]
         mn=m*nn
@@ -162,7 +213,7 @@
 
 def bwd_x(L,Tm,DX,s,r0,n):
     rows=pl.ds(r0,n)
-    DX[rows,:]=Tm['EM'][rows,:]+halves(mm(Tm['FKV'][rows,:],L['WKVT'][...])+mm(Tm['EO'][rows,:],L['UT2'][s]))
+    DX[rows,:]=Tm['EM'][rows,:]+halves(nt(Tm['FKV'][rows,:],L['WKVT'][...])+nt(Tm['EO'][rows,:],L['UT2'][s]))
 
 
 MESH = pl.DeviceIdType.MESH
@@ -171,10 +222,13 @@
 VECS = ((4, BQ), (5, BK), (6, BV), (7, BO), (8, GK), (9, SK), (10, GV), (11, SV), (15, BD), (13, BU0))
 SMALL = 16
 GROUPS = (
-    ((1, "up"), (1, "dn"), (1, "q"), (1, "o"), (1, "k"), (1, "v"), (1, "small")),
-    ((0, "up"), (0, "dn"), (0, "q"), (0, "o")),
+    ((1, "up"), (1, "dn"), (1, "q"), (1, "o")),
+    ((1, "k"), (1, "v"), (1, "small")),
+    ((0, "up"), (0, "dn")),
+    ((0, "q"), (0, "o")),
     ((0, "k"), (0, "v"), (0, "small")),
 )
+NG = len(GROUPS)
 
 
 def shard(name, n_zero):
@@ -199,18 +253,6 @@
     return places, sizes, pieces
 
 
-def center(x, a1):
-    h = x.astype(BF)
-    r = x - h.astype(F32)
-    m = r.astype(BF)
-    lo = (r - m.astype(F32)).astype(BF)
-    return x - (mm(h, a1) + mm(m, a1) + mm(lo, a1))
-
-
-def one(x):
-    return jnp.sum(x, axis=0, keepdims=True)
-
-
 class Names:
     pass
 
@@ -232,6 +274,8 @@
     for k in range(1, n_dp):
         pl.semaphore_signal(barrier, inc=1, device_id=(dpeer[k], zero), device_id_type=MESH)
 
+    len_in = pltpu.make_async_copy(R.lengths_in, R.lengths, R.io_sem.at[2])
+    len_in.start()
     small_in = []
     for i, (arg, _) in enumerate(VECS):
         c = pltpu.make_async_copy(R.params[arg], R.stage[i], R.stage_sem.at[i])
@@ -312,9 +356,7 @@
 
     for k in range(1, n_zero):
         vec_copy(k).start()
-    send_weights(0, ("q", "o", "up", "dn"))
-    send_weights(1, NAMES)
-
+    len_in.wait()
     gm = group_mask()
     a = jnp.where(gm, 1.0 / HD, 0.0).astype(BF)
     R.A2[0:D, :] = a
@@ -331,9 +373,20 @@
 
     Ls, Tm = R.layers, R.temps
     Tm["A2"] = R.A2
+    R.Y[TOK:, :] = jnp.zeros((R.Y.shape[0] - TOK, D), F32)
     nodes_in.wait()
     for s in range(SEGS):
-        Ls[0]["H"][s * BLK : (s + 1) * BLK, :] = R.nodes_v[pl.ds(st[s], BLK), :]
+        x = R.nodes_v[pl.ds(st[s], BLK), :]
+        Ls[0]["H"][s * BLK : (s + 1) * BLK, :] = x
+        Ls[0]["X"][s * BLK : (s + 1) * BLK, :] = pack(x)
+    send_weights(0, ("q", "o"))
+    cot_in.wait()
+    sum_e = zero8 = jnp.zeros((8, D), F32)
+    for s in range(SEGS):
+        x = jnp.where(live(s * BLK, BLK), R.cot_v[pl.ds(st[s], BLK), :], 0.0)
+        Tm["E"][s * BLK : (s + 1) * BLK, :] = x
+        Tm["ED"][s * BLK : (s + 1) * BLK, :] = pack(x)
+        sum_e = sum_e + part(x)
 
     for k in range(1, n_zero):
         vec_copy(k).wait_recv()
@@ -345,27 +398,45 @@
         R.vec[level] = x
         vecs.append(R.vec.at[level])
 
+    tiles = [(s, s * BLK) for s in range(SEGS)]
+
+    def pipe(stages):
+        kept = [None] * len(tiles)
+        for t in range(len(tiles) + len(stages) - 1):
+            for j, stage in enumerate(stages):
+                if 0 <= t - j < len(tiles):
+                    kept[t - j] = stage(tiles[t - j], kept[t - j])
+        return kept
+
     for level in range(2):
-        L = Ls[level]
+        L, vec = Ls[level], vecs[level]
         dst = Ls[1]["H"] if level == 0 else R.Y
         w = {n: R.weights[n].at[level] for n in NAMES}
         take_weights(level, ("k", "v"))
-        prep_kv(L, w, vecs[level], R.A2)
-        for s in range(SEGS):
-            fwd_a(L, vecs[level], R.A2, live, s * BLK, BLK)
+        if level == 0:
+            send_weights(0, ("up", "dn"))
+        prep_kv(L, w, vec, R.A2)
+        for s, r in tiles:
+            fwd_a(L, vec, R.A2, live, r, BLK, level == 1)
         take_weights(level, ("q", "o"))
-        prep_qo(L, w)
-        for s in range(SEGS):
-            fwd_s(L, vecs[level], gm, s, inv[s])
+        if level == 0:
+            send_weights(1, NAMES)
+        prep_qo(L, w, vec)
+        fwd_s(L, vec, gm, inv)
         take_weights(level, ("up", "dn"))
         prep_ff(L, w)
-        for s in range(SEGS):
-            fwd_c(L, vecs[level], dst, s, s * BLK, BLK)
-
-    cot_in.wait()
-    for s in range(SEGS):
-        x = R.cot_v[pl.ds(st[s], BLK), :]
-        Tm["E"][s * BLK : (s + 1) * BLK, :] = jnp.where(live(s * BLK, BLK), x, 0.0)
+
+        def middle(tile, _):
+            return fwd_c1(L, *tile, BLK)
+
+        def hidden(tile, mid):
+            fwd_c2(L, vec, tile[1], BLK)
+            return mid
+
+        def close(tile, mid):
+            fwd_c3(L, vec, dst, mid, tile[1], BLK)
+
+        pipe([middle, hidden, close])
 
     def put(level, name, g):
         grp, at = places[level, name]
@@ -441,7 +512,7 @@
     def end_final(grp):
         for k in range(1, n_dp):
             final_copy(grp, k, dfrom[k]).wait_recv()
-        c = pltpu.make_async_copy(R.gfin[grp], R.fin_out[grp], R.io_sem.at[4 + grp])
+        c = pltpu.make_async_copy(R.gfin[grp], R.fin_out[grp], R.io_sem.at[5 + grp])
         c.start()
         return c
 
@@ -459,72 +530,81 @@
                     x = jnp.where((it >= st[s]) & (it < st[s + 1]), y, x)
             o[t0 : t0 + step, :] = x
 
-    R.Y[TOK:, :] = jnp.zeros((R.Y.shape[0] - TOK, D), F32)
     unpack(R.nodes_v, R.nodes_v)
-    store_out = pltpu.make_async_copy(R.nodes_v, R.out, R.io_sem.at[2])
+    store_out = pltpu.make_async_copy(R.nodes_v, R.out, R.io_sem.at[3])
     store_out.start()
 
-    zero8 = jnp.zeros((8, D), F32)
     for level in (1, 0):
-        L = Ls[level]
+        L, vec = Ls[level], vecs[level]
         w = {n: R.weights[n].at[level] for n in NAMES}
         prep_back(L, w)
-        sb, su, sc = zero8, jnp.zeros((8, FF), F32), []
-        for s in range(SEGS):
-            b, u, o = bwd_a(L, Tm, s * BLK, BLK)
-            sb, su = sb + b, su + u
-            sc.append(o)
-        if level == 0:
-            start_dp(0)
+
+        def feed(tile, _):
+            return bwd_a1(L, Tm, tile[1], BLK, level == 0)
+
+        def after(tile, sums):
+            return (*sums, bwd_a2(L, Tm, tile[1], BLK))
+
+        sums = pipe([feed, after])
+        sb = sum_e if level == 1 else sum((x[0] for x in sums), zero8)
+        su = sum((x[1] for x in sums), jnp.zeros((8, FF), F32))
+        sc = [x[2] for x in sums]
         put(level, "dn", quads(tn(L["ACT"][...], Tm["ED"][...])))
         put(level, "up", quads(tn(L["MD"][...], Tm["EP"][...])))
-        gq = go = jnp.zeros((D, D), F32)
-        gbq = zero8
-        es = []
-        for s in range(SEGS):
-            eT, e2, q1, b1, o1 = bwd_s(L, vecs[level], Tm, gm, s, inv[s], sc[s])
-            gq, go, gbq = gq + q1, go + o1, gbq + b1
-            es.append((eT, e2))
+        if level == 0:
+            start_zero(2)
+        hs = bwd_s1(L, Tm, sc)
+        pp = bwd_s2(L, hs)
+        es = bwd_s3(L, gm, inv, pp)
+        gq, gbq, go = bwd_s4(L, hs, pp)
         put(level, "q", gq)
         put(level, "o", go)
         if level == 0:
-            start_zero(1)
+            start_zero(3)
+            start_dp(0)
+        else:
+            start_zero(0)
         ss = [zero8] * 6
-        for s in range(SEGS):
-            o = bwd_b(L, vecs[level], Tm, R.A2, *es[s], s * BLK, BLK)
+        for s, r in tiles:
+            o = bwd_b(L, vec, Tm, R.A2, *es[s], r, BLK)
             ss = [x + y for x, y in zip(ss, o)]
         a1 = R.A2[0:D, :]
         gkv = tn(L["X"][...], Tm["FKV"][...])
         gkv = gkv[0:D] + gkv[D:]
         put(level, "k", center(halves(gkv[:, : 2 * D]), a1))
         put(level, "v", center(halves(gkv[:, 2 * D :]), a1))
-        rows = [None] * SMALL
-        rows[BQ], rows[BK], rows[BV] = one(gbq), one(center(ss[2], a1)), one(center(ss[5], a1))
+        rows = [jnp.zeros((1, D), F32)] * SMALL
+        rows[BQ], rows[BK], rows[BV] = gbq, one(center(ss[2], a1)), one(center(ss[5], a1))
         rows[BO] = one(sc[0] + sc[1] + sc[2] + sc[3])
         rows[SK], rows[GK], rows[SV], rows[GV] = one(ss[0]), one(ss[1]), one(ss[3]), one(ss[4])
         rows[BD] = one(sb)
         u = one(su)
         rows[BU0], rows[BU1] = u[:, :D], u[:, D:]
-        rows = [jnp.zeros((1, D), F32) if r is None else r for r in rows]
         small = jnp.concatenate(rows, axis=0)
         grp, at = places[level, "small"]
         for p in range(n_zero):
             R.gsend[grp][p, at : at + SMALL, :] = small
-        start_zero(0 if level == 1 else 2)
-        if level == 0:
+        if level == 1:
+            start_zero(1)
+        else:
+            start_zero(4)
+            start_dp(1)
             start_final(0)
         dst = Tm["E"] if level == 1 else R.Y
-        for s in range(SEGS):
-            bwd_x(L, Tm, dst, s, s * BLK, BLK)
-
-    start_dp(1)
+        for s, r in tiles:
+            bwd_x(L, Tm, dst, s, r, BLK)
+
     start_dp(2)
+    start_dp(3)
     unpack(R.cot_v, R.cot_v)
-    store_gx = pltpu.make_async_copy(R.cot_v, R.gx, R.io_sem.at[3])
+    store_gx = pltpu.make_async_copy(R.cot_v, R.gx, R.io_sem.at[4])
     store_gx.start()
+    start_dp(4)
     start_final(1)
     start_final(2)
-    last = [store_out, store_gx] + [end_final(g) for g in range(3)]
+    start_final(3)
+    start_final(4)
+    last = [store_out, store_gx] + [end_final(g) for g in range(NG)]
 
     for level in range(2):
         for name in NAMES:
@@ -532,7 +612,7 @@
                 weight_copy(level, name, k, zero).wait_send()
     for k in range(1, n_zero):
         vec_copy(k).wait_send()
-    for g in range(3):
+    for g in range(NG):
         for k in range(1, n_zero):
             zero_copy(g, k).wait_send()
         for k in range(1, n_dp):
@@ -554,17 +634,16 @@
         c.start()
         copies.append(c)
 
-    fins = []
-    for g in range(3):
-        c = pltpu.make_async_copy(R.fin[g], R.fin_v[g], R.fin_sem.at[g])
+    smalls = []
+    for level in range(2):
+        g, at = places[level, "small"]
+        c = pltpu.make_async_copy(R.fin[g].at[pl.ds(at, SMALL), :], R.small.at[level], R.small_sem.at[level])
         c.start()
-        fins.append(c)
+        smalls.append(c)
     half = TOK // 2
     for i in range(2):
         copy(R.out.at[pl.ds(i * half, half), :], R.outs[0].at[pl.ds(i * half, half), :])
         copy(R.gx.at[pl.ds(i * half, half), :], R.outs[1].at[pl.ds(i * half, half), :])
-    for c in fins:
-        c.wait()
     for name, arg in ARG.items():
         for level in range(2):
             g, at = places[level, name]
@@ -572,16 +651,15 @@
             if name == "up":
                 for h in range(2):
                     copy(
-                        R.fin_v[g].at[pl.ds(at + h * n, n), :],
+                        R.fin[g].at[pl.ds(at + h * n, n), :],
                         R.outs[2 + arg].at[level, :, pl.ds(h * D, D)],
                     )
             else:
-                copy(R.fin_v[g].at[pl.ds(at, n), :], R.outs[2 + arg].at[level])
+                copy(R.fin[g].at[pl.ds(at, n), :], R.outs[2 + arg].at[level])
     zero = lax.axis_index("zero")
-    small = []
-    for level in range(2):
-        g, at = places[level, "small"]
-        small.append(R.fin_v[g][at : at + SMALL, :])
+    for c in smalls:
+        c.wait()
+    small = [R.small[level] for level in range(2)]
     for arg, row in VECS:
         n = R.outs[2 + arg].shape[1]
         x = jnp.concatenate([s[row : row + 1, :] for s in small], axis=0)
@@ -604,17 +682,15 @@
         order.append(name)
         scratch.append(shape)
 
-    def sds(*shape):
-        return jax.ShapeDtypeStruct(shape, F32)
-
     n_params = len(params)
-    out_shape = [sds(TOK, D), sds(TOK, D)] + [sds(n_dp, p, D) for p in pieces]
+    out_shape = [VM((TOK, D), F32)] * 2 + [VM((n_dp, p, D), F32) for p in pieces]
     ls, ts = list(LAYER_SCRATCH), [n for n in TMP_SCRATCH if n != "A2"]
     for level in range(2):
         for n in ls:
             add(("layer", level, n), VM(*LAYER_SCRATCH[n]))
     for n in ts:
         add(("temp", n), VM(*TMP_SCRATCH[n]))
+    add("lengths", pltpu.SMEM((SEGS,), jnp.int32))
     add("A2", VM(*TMP_SCRATCH["A2"]))
     add("Y", VM((TOK + 768, D), F32))
     add("nodes_v", VM((TOK, D), F32))
@@ -627,33 +703,33 @@
     add("vec_own", VM((2, SMALL, D), F32))
     add("vec_in", VM((n_zero - 1, 2, SMALL, D), F32))
     add("vec", VM((2, SMALL, D), F32))
-    for g in range(3):
+    for g in range(NG):
         add(("gsend", g), VM((n_zero, sizes[g], D), F32))
         add(("gzero", g), VM((n_zero - 1, sizes[g], D), F32))
         add(("gred", g), VM((n_dp, pieces[g], D), F32))
         add(("gdp", g), VM((n_dp - 1, pieces[g], D), F32))
         add(("gfin", g), VM((n_dp, pieces[g], D), F32))
     add("stage_sem", dma((len(VECS),)))
-    add("io_sem", dma((8,)))
+    add("io_sem", dma((5 + NG,)))
     add("own_sem", dma((2, 6)))
     add("w_send", dma((2, 6, n_zero - 1)))
     add("w_recv", dma((2, 6, n_zero - 1)))
     add("vec_send", dma((n_zero - 1,)))
     add("vec_recv", dma((n_zero - 1,)))
     for n, m in (("z", n_zero), ("d", n_dp), ("f", n_dp)):
-        add(n + "_send", dma((3, m - 1)))
-        add(n + "_recv", dma((3, m - 1)))
+        add(n + "_send", dma((NG, m - 1)))
+        add(n + "_recv", dma((NG, m - 1)))
 
     def body(*refs):
-        lengths, nodes, cot = refs[:3]
+        lengths_in, nodes, cot = refs[:3]
         pr = refs[3 : 3 + n_params]
-        outs = refs[3 + n_params : 8 + n_params]
-        rest = refs[8 + n_params :]
-        simple = dict(lengths=lengths, nodes=nodes, cotangent=cot, params=pr, out=outs[0], gx=outs[1], fin_out=outs[2:5])
+        outs = refs[3 + n_params : 5 + NG + n_params]
+        rest = refs[5 + NG + n_params :]
+        simple = dict(lengths_in=lengths_in, nodes=nodes, cotangent=cot, params=pr, out=outs[0], gx=outs[1], fin_out=outs[2:])
         layers, temps = [{}, {}], {}
         simple.update(layers=layers, temps=temps, stage=[None] * len(VECS), weights={})
         for n in ("gsend", "gzero", "gred", "gdp", "gfin"):
-            simple[n] = [None] * 3
+            simple[n] = [None] * NG
         for key, ref in zip(order, rest):
             if isinstance(key, str):
                 simple[key] = ref
@@ -668,11 +744,11 @@
     call = pl.pallas_call(
         body,
         out_shape=out_shape,
-        in_specs=[pl.BlockSpec(memory_space=pltpu.SMEM)] + [any_] * (2 + n_params),
-        out_specs=[any_] * 5,
+        in_specs=[any_] * (3 + n_params),
+        out_specs=[any_] * (2 + NG),
         scratch_shapes=scratch,
         compiler_params=pltpu.CompilerParams(
-            collective_id=0, has_side_effects=True, vmem_limit_bytes=60 * 1024 * 1024
+            collective_id=0, has_side_effects=True, vmem_limit_bytes=56 * 1024 * 1024
         ),
     )
     return call
@@ -680,7 +756,7 @@
 
 def make_finish(n_dp, n_zero, params):
     places, sizes, pieces = group_layout(n_dp, n_zero)
-    any_ = pl.BlockSpec(memory_space=pltpu.HBM)
+    any_ = pl.BlockSpec(memory_space=pl.ANY)
     vmem = pl.BlockSpec(memory_space=pltpu.VMEM)
     out_shape = [jax.ShapeDtypeStruct((TOK, D), F32)] * 2
     out_shape += [jax.ShapeDtypeStruct(p.shape, F32) for p in params]
@@ -689,21 +765,25 @@
 
     def body(*refs):
         out, gx = refs[:2]
-        fin = refs[2:5]
-        outs = refs[5 : 7 + len(params)]
-        rest = refs[7 + len(params) :]
-        simple = dict(out=out, gx=gx, fin=fin, outs=outs, fin_v=rest[:3], sem=rest[3], fin_sem=rest[4])
+        fin = refs[2 : 2 + NG]
+        outs = refs[2 + NG : 4 + NG + len(params)]
+        rest = refs[4 + NG + len(params) :]
+        simple = dict(out=out, gx=gx, fin=fin, outs=outs, small=rest[0], sem=rest[1], small_sem=rest[2])
         finish_kernel(n_dp, n_zero, list(simple), *simple.values())
 
-    return pl.pallas_call(
+    call = pl.pallas_call(
         body,
         out_shape=out_shape,
-        in_specs=[any_] * 5,
+        in_specs=[any_] * (2 + NG),
         out_specs=out_specs,
-        scratch_shapes=[VM((n_dp * p, D), F32) for p in pieces]
-        + [pltpu.SemaphoreType.DMA((18,)), pltpu.SemaphoreType.DMA((3,))],
-        compiler_params=pltpu.CompilerParams(vmem_limit_bytes=32 * 1024 * 1024),
+        scratch_shapes=[
+            VM((2, SMALL, D), F32),
+            pltpu.SemaphoreType.DMA((18,)),
+            pltpu.SemaphoreType.DMA((2,)),
+        ],
+        compiler_params=pltpu.CompilerParams(vmem_limit_bytes=16 * 1024 * 1024),
     )
+    return lambda *xs: call(*[pltpu.with_memory_space_constraint(x, pltpu.VMEM) for x in xs])
 
 
 def solution(mesh):

time: 70.8 us -> 56.8 us (0.80)
  Pallas kernels: 64.6 us -> 55.8 us
  local copies, waits for them, and re-layouts: 5.09 us -> 0 us
    pallas_call x1, Pallas kernels: 61.9 us -> 53.6 us  [local(): make_fused(n_dp, n_zero, params)(lengths, nodes, cotangent, *params)]
    unnamed x10 -> x0, local copies, waits for them, and re-layouts: 5.09 us -> none
where the time goes in v2:
time: 56.8 us; the launch traced here: 56.7 us
  Pallas kernels  55.8 us (98%)
  between operations  0.83 us (1%)
    pallas_call x1, Pallas kernels, local(): make_fused(n_dp, n_zero, params)(lengths, nodes, cotangent, *params)  53.6 us
    pallas_call x1, Pallas kernels, make_finish(): call(*[pltpu.with_memory_space_constraint(x, pltpu.VMEM) for x in xs])  2.2 us

profile of v2, /device:TPU:0, one launch (start us, length us, event | category | flops | bytes accessed | tf_op | source)
XLA Modules:
  0.0 56.7 jit_solution(947007665356282932)
XLA Ops:
  0.7 53.6 %shard_map.322 = (f32[2048,128]{1,0:T(8,128)S(1)}, f32[2048,128]{1,0:T(8,128)S(1)}, f32[8,24,128]{2,1,0:T(8,128)S(1)}, f32[8,16,128]{2,1,0:T(8,128)S(1)}, f32[8,...) custom-call(s32[4]{0:T(128)} %refs_0_.1, f32[2048,128]{1,0:T(8,128)} %refs_1_.1, ...), custom_call_target="tpu_custom_call" | custom-call | tf_op jit(solution)/shard_map/pallas_call | solution.py:796
  54.3 2.2 %shard_map.323 = (f32[2048,128]{1,0:T(8,128)}, f32[2048,128]{1,0:T(8,128)}, f32[2,32,128]{2,1,0:T(8,128)}, f32[2,32,128]{2,1,0:T(8,128)}, f32[2,32,128]{2,1,0:T(...) custom-call(f32[2048,128]{1,0:T(8,128)S(1)} %get-tuple-element.25.re, ...), custom_call_target="tpu_custom_call" | custom-call | tf_op jit(solution)/shard_map/pallas_call | solution.py:786

commit v3 on v2

--- a/solution.py
+++ b/solution.py
@@ -196,20 +196,17 @@
     gq=gq[:AUG]+gq[AUG:]
     return gq[:D],gq[D:D+1],go
 
-def bwd_b(L,vec,Tm,A2,esT2,es2,r0,n):
+def bwd_b(L,vec,Tm,A2,es,r0,n,i):
     rows=pl.ds(r0,n)
-    a2=A2[...]
-    out=[]
-    for i,(N,R,O,g,f,w) in enumerate((('NK','RK','VN',GK,nt,esT2),('NV','RV','KN',GV,mm,es2))):
-        en=halves(f(L[O][rows,:],w))
-        nn=L[N][rows,:]
-        m=en*vec[g:g+1,:]
-        mn=m*nn
-        av=mm(pack(mn),a2)
-        f=L[R][rows,:]*(m-nn*av)
-        Tm['FKV'][rows,i*2*D:(i+1)*2*D]=pack(f)
-        out+= [part(en),part(en*nn),part(f)]
-    return out
+    N,R,O,g,dot=(('NK','RK','VN',GK,nt),('NV','RV','KN',GV,mm))[i]
+    en=halves(dot(L[O][rows,:],es))
+    nn=L[N][rows,:]
+    m=en*vec[g:g+1,:]
+    mn=m*nn
+    av=mm(pack(mn),A2[...])
+    f=L[R][rows,:]*(m-nn*av)
+    Tm['FKV'][rows,i*2*D:(i+1)*2*D]=pack(f)
+    return part(en),part(en*nn),part(f)
 
 def bwd_x(L,Tm,DX,s,r0,n):
     rows=pl.ds(r0,n)
@@ -222,12 +219,16 @@
 VECS = ((4, BQ), (5, BK), (6, BV), (7, BO), (8, GK), (9, SK), (10, GV), (11, SV), (15, BD), (13, BU0))
 SMALL = 16
 GROUPS = (
-    ((1, "up"), (1, "dn"), (1, "q"), (1, "o")),
-    ((1, "k"), (1, "v"), (1, "small")),
-    ((0, "up"), (0, "dn")),
-    ((0, "q"), (0, "o")),
-    ((0, "k"), (0, "v"), (0, "small")),
+    (((1, "up"), (1, "dn")), True),
+    (((1, "q"), (1, "o")), True),
+    (((1, "k"), (1, "v"), (1, "small")), True),
+    (((0, "up"), (0, "dn")), True),
+    (((0, "q"), (0, "o")), True),
+    (((0, "k"),), False),
+    (((0, "small"),), True),
+    (((0, "v"),), False),
 )
+PAIR = 2
 NG = len(GROUPS)
 
 
@@ -237,9 +238,9 @@
     return D // n_zero, FF if name == "up" else D
 
 
-def group_layout(n_dp, n_zero):
+def group_layout(n_zero):
     places, sizes, pieces = {}, [], []
-    for g, members in enumerate(GROUPS):
+    for g, (members, halved) in enumerate(GROUPS):
         at = 0
         for item in members:
             places[item] = (g, at)
@@ -248,8 +249,9 @@
             else:
                 rows, cols = shard(item[1], n_zero)
                 at += rows * cols // D
+        at = -(-at // 16) * 16
         sizes.append(at)
-        pieces.append(-(-at // (8 * n_dp)) * 8)
+        pieces.append(at // PAIR if halved else at)
     return places, sizes, pieces
 
 
@@ -261,18 +263,29 @@
     R = Names()
     for name, ref in zip(order, refs):
         setattr(R, name, ref)
-    places, sizes, pieces = group_layout(n_dp, n_zero)
+    places, sizes, pieces = group_layout(n_zero)
     dp, zero = lax.axis_index("dp"), lax.axis_index("zero")
     zpeer = [None] + [lax.rem(zero + k, n_zero) for k in range(1, n_zero)]
-    zfrom = [None] + [lax.rem(zero + n_zero - k, n_zero) for k in range(1, n_zero)]
-    dpeer = [None] + [lax.rem(dp + k, n_dp) for k in range(1, n_dp)]
-    dfrom = [None] + [lax.rem(dp + n_dp - k, n_dp) for k in range(1, n_dp)]
+    fast, slow, n_slow = lax.rem(dp, PAIR), dp // PAIR, n_dp // PAIR
+    n_plane = PAIR * n_zero
+    me = fast * n_zero + zero
+    ppeer = [None] + [lax.rem(me + k, n_plane) for k in range(1, n_plane)]
+    speer = [None] + [lax.rem(slow + k, n_slow) for k in range(1, n_slow)]
+    sfrom = [None] + [lax.rem(slow + n_slow - k, n_slow) for k in range(1, n_slow)]
+    pfrom = [None] + [lax.rem(me + n_plane - k, n_plane) for k in range(1, n_plane)]
+    other = PAIR - 1 - fast
+
+    def in_plane(k):
+        return (slow * PAIR + ppeer[k] // n_zero, lax.rem(ppeer[k], n_zero))
+
+    def along(k):
+        return (speer[k] * PAIR + fast, zero)
 
     barrier = pltpu.get_barrier_semaphore()
-    for k in range(1, n_zero):
-        pl.semaphore_signal(barrier, inc=1, device_id=(dp, zpeer[k]), device_id_type=MESH)
-    for k in range(1, n_dp):
-        pl.semaphore_signal(barrier, inc=1, device_id=(dpeer[k], zero), device_id_type=MESH)
+    for k in range(1, n_slow):
+        pl.semaphore_signal(barrier, inc=1, device_id=along(k), device_id_type=MESH)
+    for k in range(1, n_plane):
+        pl.semaphore_signal(barrier, inc=1, device_id=in_plane(k), device_id_type=MESH)
 
     len_in = pltpu.make_async_copy(R.lengths_in, R.lengths, R.io_sem.at[2])
     len_in.start()
@@ -302,29 +315,67 @@
     cot_in = pltpu.make_async_copy(R.cotangent, R.cot_v, R.io_sem.at[1])
     cot_in.start()
 
-    pl.semaphore_wait(barrier, n_zero - 1 + n_dp - 1)
-
-    def weight_copy(level, name, k, who):
-        i = NAMES.index(name)
+    pl.semaphore_wait(barrier, n_slow - 1 + n_plane - 1)
+
+    n_x = n_zero // 2
+    mate = zero + 1 - 2 * lax.rem(zero, 2)
+    xpeer = [None] + [lax.rem(zero + 2 * k, n_zero) for k in range(1, n_x)]
+    xfrom = [None] + [lax.rem(zero + n_zero - 2 * k, n_zero) for k in range(1, n_x)]
+    mate_from = [None] + [lax.rem(mate + n_zero - 2 * k, n_zero) for k in range(1, n_x)]
+
+    def part_of(level, name, who):
+        if name == "vec":
+            return R.vec_in.at[who]
+        return R.weights[name].at[level, rows_of(name, who), :]
+
+    def own_part(level, name):
+        return R.vec_own if name == "vec" else R.params[ARG[name]].at[level]
+
+    def place(level, name):
+        return 12 if name == "vec" else level * 6 + NAMES.index(name)
+
+    def x_copy(level, name, k, who):
+        i = place(level, name)
         return pltpu.make_async_remote_copy(
-            src_ref=R.params[ARG[name]].at[level],
-            dst_ref=R.weights[name].at[level, rows_of(name, who), :],
-            send_sem=R.w_send.at[level, i, k - 1],
-            recv_sem=R.w_recv.at[level, i, k - 1],
-            device_id=(dp, zpeer[k]),
+            src_ref=own_part(level, name),
+            dst_ref=part_of(level, name, who),
+            send_sem=R.x_send.at[i, k - 1],
+            recv_sem=R.x_recv.at[i, k - 1],
+            device_id=(dp, xpeer[k]),
             device_id_type=MESH,
         )
 
+    def mate_copy(level, name, k, who):
+        i = place(level, name)
+        return pltpu.make_async_remote_copy(
+            src_ref=own_part(level, name) if k == 0 else part_of(level, name, xfrom[k]),
+            dst_ref=part_of(level, name, who),
+            send_sem=R.m_send.at[i, k],
+            recv_sem=R.m_recv.at[i, k],
+            device_id=(dp, mate),
+            device_id_type=MESH,
+        )
+
     def send_weights(level, names):
         for name in names:
-            for k in range(1, n_zero):
-                weight_copy(level, name, k, zero).start()
+            for k in range(1, n_x):
+                x_copy(level, name, k, zero).start()
+        for name in names:
+            mate_copy(level, name, 0, zero).start()
+
+    def relay_weights(level, names):
+        for name in names:
+            for k in range(1, n_x):
+                x_copy(level, name, k, xfrom[k]).wait_recv()
+                mate_copy(level, name, k, xfrom[k]).start()
 
     def take_weights(level, names):
         for name in names:
-            own[level, name].wait()
-            for k in range(1, n_zero):
-                weight_copy(level, name, k, zfrom[k]).wait_recv()
+            if name != "vec":
+                own[level, name].wait()
+            mate_copy(level, name, 0, mate).wait_recv()
+            for k in range(1, n_x):
+                mate_copy(level, name, k, mate_from[k]).wait_recv()
 
     send_weights(0, ("k", "v"))
 
@@ -344,18 +395,8 @@
             R.vec_own[:, row, :] = jnp.where(first, x, 0.0)
             R.vec_own[:, row + 1, :] = jnp.where(first, 0.0, x)
 
-    def vec_copy(k):
-        return pltpu.make_async_remote_copy(
-            src_ref=R.vec_own,
-            dst_ref=R.vec_in.at[k - 1],
-            send_sem=R.vec_send.at[k - 1],
-            recv_sem=R.vec_recv.at[k - 1],
-            device_id=(dp, zpeer[k]),
-            device_id_type=MESH,
-        )
-
-    for k in range(1, n_zero):
-        vec_copy(k).start()
+    send_weights(0, ("vec",))
+
     len_in.wait()
     gm = group_mask()
     a = jnp.where(gm, 1.0 / HD, 0.0).astype(BF)
@@ -373,13 +414,13 @@
 
     Ls, Tm = R.layers, R.temps
     Tm["A2"] = R.A2
-    R.Y[TOK:, :] = jnp.zeros((R.Y.shape[0] - TOK, D), F32)
+    for y in (R.Y, R.Y2):
+        y[TOK:, :] = jnp.zeros((y.shape[0] - TOK, D), F32)
     nodes_in.wait()
     for s in range(SEGS):
         x = R.nodes_v[pl.ds(st[s], BLK), :]
         Ls[0]["H"][s * BLK : (s + 1) * BLK, :] = x
         Ls[0]["X"][s * BLK : (s + 1) * BLK, :] = pack(x)
-    send_weights(0, ("q", "o"))
     cot_in.wait()
     sum_e = zero8 = jnp.zeros((8, D), F32)
     for s in range(SEGS):
@@ -388,24 +429,28 @@
         Tm["ED"][s * BLK : (s + 1) * BLK, :] = pack(x)
         sum_e = sum_e + part(x)
 
-    for k in range(1, n_zero):
-        vec_copy(k).wait_recv()
+    send_weights(0, ("q", "o", "up", "dn"))
+    relay_weights(0, ("k", "v", "vec"))
+    send_weights(1, NAMES)
+    take_weights(0, ("vec",))
     vecs = []
     for level in range(2):
         x = R.vec_own[level]
         for k in range(1, n_zero):
-            x = x + R.vec_in[k - 1, level]
+            x = x + R.vec_in[zpeer[k], level]
         R.vec[level] = x
         vecs.append(R.vec.at[level])
 
     tiles = [(s, s * BLK) for s in range(SEGS)]
 
-    def pipe(stages):
+    def pipe(stages, hook=None):
         kept = [None] * len(tiles)
         for t in range(len(tiles) + len(stages) - 1):
             for j, stage in enumerate(stages):
                 if 0 <= t - j < len(tiles):
                     kept[t - j] = stage(tiles[t - j], kept[t - j])
+            if hook is not None and t == 2:
+                hook()
         return kept
 
     for level in range(2):
@@ -413,19 +458,16 @@
         dst = Ls[1]["H"] if level == 0 else R.Y
         w = {n: R.weights[n].at[level] for n in NAMES}
         take_weights(level, ("k", "v"))
-        if level == 0:
-            send_weights(0, ("up", "dn"))
         prep_kv(L, w, vec, R.A2)
         for s, r in tiles:
             fwd_a(L, vec, R.A2, live, r, BLK, level == 1)
+            if level == 0 and s == 0:
+                relay_weights(0, ("q", "o", "up", "dn"))
         take_weights(level, ("q", "o"))
-        if level == 0:
-            send_weights(1, NAMES)
         prep_qo(L, w, vec)
         fwd_s(L, vec, gm, inv)
         take_weights(level, ("up", "dn"))
         prep_ff(L, w)
-
         def middle(tile, _):
             return fwd_c1(L, *tile, BLK)
 
@@ -436,7 +478,7 @@
         def close(tile, mid):
             fwd_c3(L, vec, dst, mid, tile[1], BLK)
 
-        pipe([middle, hidden, close])
+        pipe([middle, hidden, close], (lambda: relay_weights(1, NAMES)) if level == 0 else None)
 
     def put(level, name, g):
         grp, at = places[level, name]
@@ -449,76 +491,79 @@
             else:
                 R.gsend[grp][p, at : at + n, :] = part_p
 
-    def zero_copy(grp, k):
+    def plane_copy(grp, k, who):
+        rows, src = pieces[grp], R.gsend[grp].at[lax.rem(ppeer[k], n_zero)]
+        if GROUPS[grp][1]:
+            src = src.at[pl.ds(pl.multiple_of(ppeer[k] // n_zero * rows, 8), rows), :]
         return pltpu.make_async_remote_copy(
-            src_ref=R.gsend[grp].at[zpeer[k]],
-            dst_ref=R.gzero[grp].at[k - 1],
-            send_sem=R.z_send.at[grp, k - 1],
-            recv_sem=R.z_recv.at[grp, k - 1],
-            device_id=(dp, zpeer[k]),
+            src_ref=src,
+            dst_ref=R.gplane[grp].at[who],
+            send_sem=R.p_send.at[grp, k - 1],
+            recv_sem=R.p_recv.at[grp, k - 1],
+            device_id=in_plane(k),
             device_id_type=MESH,
         )
 
-    def start_zero(grp):
-        for k in range(1, n_zero):
-            zero_copy(grp, k).start()
-
-    def piece_copy(grp, k):
+    def slow_copy(grp, k, who):
         return pltpu.make_async_remote_copy(
-            src_ref=R.gred[grp].at[dpeer[k]],
-            dst_ref=R.gdp[grp].at[k - 1],
-            send_sem=R.d_send.at[grp, k - 1],
-            recv_sem=R.d_recv.at[grp, k - 1],
-            device_id=(dpeer[k], zero),
+            src_ref=R.gslow[grp].at[slow],
+            dst_ref=R.gslow[grp].at[who],
+            send_sem=R.s_send.at[grp, k - 1],
+            recv_sem=R.s_recv.at[grp, k - 1],
+            device_id=along(k),
             device_id_type=MESH,
         )
 
-    def final_copy(grp, k, who):
+    def half_of(grp, who):
+        rows = pieces[grp]
+        return R.fin_out[grp].at[pl.ds(pl.multiple_of(who * rows, 8), rows), :]
+
+    def pair_copy(grp, who):
         return pltpu.make_async_remote_copy(
-            src_ref=R.gfin[grp].at[dp],
-            dst_ref=R.gfin[grp].at[who],
-            send_sem=R.f_send.at[grp, k - 1],
-            recv_sem=R.f_recv.at[grp, k - 1],
-            device_id=(dpeer[k], zero),
+            src_ref=half_of(grp, fast),
+            dst_ref=half_of(grp, who),
+            send_sem=R.f_send.at[grp],
+            recv_sem=R.f_recv.at[grp],
+            device_id=(slow * PAIR + other, zero),
             device_id_type=MESH,
         )
 
-    def start_dp(grp):
-        for k in range(1, n_zero):
-            zero_copy(grp, k).wait_recv()
-        total, piece = sizes[grp], pieces[grp]
-        for j in range(n_dp):
-            lo, hi = j * piece, min((j + 1) * piece, total)
-            if lo < hi:
-                x = R.gsend[grp][zero, lo:hi, :]
-                for k in range(1, n_zero):
-                    x = x + R.gzero[grp][k - 1, lo:hi, :]
-                R.gred[grp][j, 0 : hi - lo, :] = x
-            if hi - lo < piece:
-                lo = max(hi - lo, 0)
-                R.gred[grp][j, lo:piece, :] = jnp.zeros((piece - lo, D), F32)
-        for k in range(1, n_dp):
-            piece_copy(grp, k).start()
-
-    def start_final(grp):
-        x = R.gred[grp][dp]
-        for k in range(1, n_dp):
-            piece_copy(grp, k).wait_recv()
-            x = x + R.gdp[grp][k - 1]
-        R.gfin[grp][dp] = x
-        for k in range(1, n_dp):
-            final_copy(grp, k, dp).start()
-
-    def end_final(grp):
-        for k in range(1, n_dp):
-            final_copy(grp, k, dfrom[k]).wait_recv()
-        c = pltpu.make_async_copy(R.gfin[grp], R.fin_out[grp], R.io_sem.at[5 + grp])
-        c.start()
-        return c
+    def start_plane(grp):
+        for k in range(1, n_plane):
+            plane_copy(grp, k, me).start()
+
+    def start_slow(grp):
+        rows = pieces[grp]
+        at = pl.multiple_of(fast * rows, 8) if GROUPS[grp][1] else 0
+        R.gplane[grp][me] = R.gsend[grp][zero, pl.ds(at, rows), :]
+        for k in range(1, n_plane):
+            plane_copy(grp, k, pfrom[k]).wait_recv()
+        x = R.gplane[grp][0]
+        for j in range(1, n_plane):
+            x = x + R.gplane[grp][j]
+        R.gslow[grp][slow] = x
+        for k in range(1, n_slow):
+            slow_copy(grp, k, slow).start()
+
+    def start_pair(grp):
+        for k in range(1, n_slow):
+            slow_copy(grp, k, sfrom[k]).wait_recv()
+        x = R.gslow[grp][0]
+        for j in range(1, n_slow):
+            x = x + R.gslow[grp][j]
+        if GROUPS[grp][1]:
+            R.fin_out[grp][pl.ds(pl.multiple_of(fast * pieces[grp], 8), pieces[grp]), :] = x
+            pair_copy(grp, fast).start()
+        else:
+            R.fin_out[grp][...] = x
+
+    def end_pair(grp):
+        if GROUPS[grp][1]:
+            pair_copy(grp, other).wait_recv()
 
     shift = [jnp.minimum(BLK * s - st[s], (BLK - 256) * s) for s in range(SEGS)]
 
-    def unpack(o, base):
+    def unpack(Y, base):
         lo, hi = (0, 256, 512, 768), (512, 1024, 1536, 2048)
         step = 256
         for t0 in range(0, TOK, step):
@@ -526,13 +571,9 @@
             x = base[t0 : t0 + step, :]
             for s in range(SEGS):
                 if t0 < hi[s] and t0 + step > lo[s]:
-                    y = R.Y[pl.ds(t0 + shift[s], step), :]
+                    y = Y[pl.ds(t0 + shift[s], step), :]
                     x = jnp.where((it >= st[s]) & (it < st[s + 1]), y, x)
-            o[t0 : t0 + step, :] = x
-
-    unpack(R.nodes_v, R.nodes_v)
-    store_out = pltpu.make_async_copy(R.nodes_v, R.out, R.io_sem.at[3])
-    store_out.start()
+            base[t0 : t0 + step, :] = x
 
     for level in (1, 0):
         L, vec = Ls[level], vecs[level]
@@ -551,28 +592,33 @@
         sc = [x[2] for x in sums]
         put(level, "dn", quads(tn(L["ACT"][...], Tm["ED"][...])))
         put(level, "up", quads(tn(L["MD"][...], Tm["EP"][...])))
+        start_plane(0 if level == 1 else 3)
         if level == 0:
-            start_zero(2)
+            start_slow(0)
         hs = bwd_s1(L, Tm, sc)
         pp = bwd_s2(L, hs)
         es = bwd_s3(L, gm, inv, pp)
         gq, gbq, go = bwd_s4(L, hs, pp)
         put(level, "q", gq)
         put(level, "o", go)
+        start_plane(1 if level == 1 else 4)
         if level == 0:
-            start_zero(3)
-            start_dp(0)
-        else:
-            start_zero(0)
+            start_slow(1)
+        a1 = R.A2[0:D, :]
         ss = [zero8] * 6
-        for s, r in tiles:
-            o = bwd_b(L, vec, Tm, R.A2, *es[s], r, BLK)
-            ss = [x + y for x, y in zip(ss, o)]
-        a1 = R.A2[0:D, :]
-        gkv = tn(L["X"][...], Tm["FKV"][...])
-        gkv = gkv[0:D] + gkv[D:]
-        put(level, "k", center(halves(gkv[:, : 2 * D]), a1))
-        put(level, "v", center(halves(gkv[:, 2 * D :]), a1))
+
+        def key_value(i):
+            for s, r in tiles:
+                o = bwd_b(L, vec, Tm, R.A2, es[s][i], r, BLK, i)
+                for j in range(3):
+                    ss[3 * i + j] = ss[3 * i + j] + o[j]
+
+        key_value(0)
+        if level == 0:
+            put(level, "k", center(quads(tn(L["X"][...], Tm["FKV"][:, : 2 * D])), a1))
+            start_plane(5)
+            start_slow(2)
+        key_value(1)
         rows = [jnp.zeros((1, D), F32)] * SMALL
         rows[BQ], rows[BK], rows[BV] = gbq, one(center(ss[2], a1)), one(center(ss[5], a1))
         rows[BO] = one(sc[0] + sc[1] + sc[2] + sc[3])
@@ -585,48 +631,60 @@
         for p in range(n_zero):
             R.gsend[grp][p, at : at + SMALL, :] = small
         if level == 1:
-            start_zero(1)
+            gkv = tn(L["X"][...], Tm["FKV"][...])
+            gkv = gkv[0:D] + gkv[D:]
+            put(level, "k", center(halves(gkv[:, : 2 * D]), a1))
+            put(level, "v", center(halves(gkv[:, 2 * D :]), a1))
+            start_plane(2)
         else:
-            start_zero(4)
-            start_dp(1)
-            start_final(0)
-        dst = Tm["E"] if level == 1 else R.Y
+            start_plane(6)
+            put(level, "v", center(quads(tn(L["X"][...], Tm["FKV"][:, 2 * D :])), a1))
+            start_plane(7)
+            start_slow(3)
+            start_pair(0)
+            start_pair(1)
+        dst = Tm["E"] if level == 1 else R.Y2
         for s, r in tiles:
             bwd_x(L, Tm, dst, s, r, BLK)
 
-    start_dp(2)
-    start_dp(3)
-    unpack(R.cot_v, R.cot_v)
+    start_slow(4)
+    start_pair(2)
+    unpack(R.Y, R.nodes_v)
+    store_out = pltpu.make_async_copy(R.nodes_v, R.out, R.io_sem.at[3])
+    store_out.start()
+    start_slow(5)
+    start_slow(6)
+    unpack(R.Y2, R.cot_v)
     store_gx = pltpu.make_async_copy(R.cot_v, R.gx, R.io_sem.at[4])
     store_gx.start()
-    start_dp(4)
-    start_final(1)
-    start_final(2)
-    start_final(3)
-    start_final(4)
-    last = [store_out, store_gx] + [end_final(g) for g in range(NG)]
-
-    for level in range(2):
-        for name in NAMES:
-            for k in range(1, n_zero):
-                weight_copy(level, name, k, zero).wait_send()
-    for k in range(1, n_zero):
-        vec_copy(k).wait_send()
+    start_slow(7)
+    for g in (3, 4, 6, 5, 7):
+        start_pair(g)
     for g in range(NG):
-        for k in range(1, n_zero):
-            zero_copy(g, k).wait_send()
-        for k in range(1, n_dp):
-            piece_copy(g, k).wait_send()
-            final_copy(g, k, dp).wait_send()
-    for c in last:
-        c.wait()
+        end_pair(g)
+
+    for level, names in ((0, NAMES + ("vec",)), (1, NAMES)):
+        for name in names:
+            mate_copy(level, name, 0, zero).wait_send()
+            for k in range(1, n_x):
+                x_copy(level, name, k, zero).wait_send()
+                mate_copy(level, name, k, xfrom[k]).wait_send()
+    for g in range(NG):
+        for k in range(1, n_plane):
+            plane_copy(g, k, me).wait_send()
+        for k in range(1, n_slow):
+            slow_copy(g, k, slow).wait_send()
+        if GROUPS[g][1]:
+            pair_copy(g, fast).wait_send()
+    store_out.wait()
+    store_gx.wait()
 
 
 def finish_kernel(n_dp, n_zero, order, *refs):
     R = Names()
     for name, ref in zip(order, refs):
         setattr(R, name, ref)
-    places, sizes, pieces = group_layout(n_dp, n_zero)
+    places, sizes, pieces = group_layout(n_zero)
     copies = []
 
     def copy(src, dst):
@@ -673,7 +731,7 @@
 
 
 def make_fused(n_dp, n_zero, params):
-    places, sizes, pieces = group_layout(n_dp, n_zero)
+    places, sizes, pieces = group_layout(n_zero)
     dma = pltpu.SemaphoreType.DMA
     any_ = pl.BlockSpec(memory_space=pl.ANY)
     order, scratch = [], []
@@ -683,7 +741,7 @@
         scratch.append(shape)
 
     n_params = len(params)
-    out_shape = [VM((TOK, D), F32)] * 2 + [VM((n_dp, p, D), F32) for p in pieces]
+    out_shape = [VM((TOK, D), F32)] * 2 + [VM((p, D), F32) for p in sizes]
     ls, ts = list(LAYER_SCRATCH), [n for n in TMP_SCRATCH if n != "A2"]
     for level in range(2):
         for n in ls:
@@ -693,6 +751,7 @@
     add("lengths", pltpu.SMEM((SEGS,), jnp.int32))
     add("A2", VM(*TMP_SCRATCH["A2"]))
     add("Y", VM((TOK + 768, D), F32))
+    add("Y2", VM((TOK + 768, D), F32))
     add("nodes_v", VM((TOK, D), F32))
     add("cot_v", VM((TOK, D), F32))
     for i, (arg, _) in enumerate(VECS):
@@ -701,24 +760,23 @@
         rows, cols = shard(n, n_zero)
         add(("weights", n), VM((2, rows * n_zero, cols), F32))
     add("vec_own", VM((2, SMALL, D), F32))
-    add("vec_in", VM((n_zero - 1, 2, SMALL, D), F32))
+    add("vec_in", VM((n_zero, 2, SMALL, D), F32))
     add("vec", VM((2, SMALL, D), F32))
     for g in range(NG):
         add(("gsend", g), VM((n_zero, sizes[g], D), F32))
-        add(("gzero", g), VM((n_zero - 1, sizes[g], D), F32))
-        add(("gred", g), VM((n_dp, pieces[g], D), F32))
-        add(("gdp", g), VM((n_dp - 1, pieces[g], D), F32))
-        add(("gfin", g), VM((n_dp, pieces[g], D), F32))
+        add(("gplane", g), VM((PAIR * n_zero, pieces[g], D), F32))
+        add(("gslow", g), VM((n_dp // PAIR, pieces[g], D), F32))
     add("stage_sem", dma((len(VECS),)))
-    add("io_sem", dma((5 + NG,)))
+    add("io_sem", dma((5,)))
     add("own_sem", dma((2, 6)))
-    add("w_send", dma((2, 6, n_zero - 1)))
-    add("w_recv", dma((2, 6, n_zero - 1)))
-    add("vec_send", dma((n_zero - 1,)))
-    add("vec_recv", dma((n_zero - 1,)))
-    for n, m in (("z", n_zero), ("d", n_dp), ("f", n_dp)):
+    for n, m in (("x", n_zero // 2 - 1), ("m", n_zero // 2)):
+        add(n + "_send", dma((13, m)))
+        add(n + "_recv", dma((13, m)))
+    for n, m in (("p", PAIR * n_zero), ("s", n_dp // PAIR)):
         add(n + "_send", dma((NG, m - 1)))
         add(n + "_recv", dma((NG, m - 1)))
+    add("f_send", dma((NG,)))
+    add("f_recv", dma((NG,)))
 
     def body(*refs):
         lengths_in, nodes, cot = refs[:3]
@@ -728,7 +786,7 @@
         simple = dict(lengths_in=lengths_in, nodes=nodes, cotangent=cot, params=pr, out=outs[0], gx=outs[1], fin_out=outs[2:])
         layers, temps = [{}, {}], {}
         simple.update(layers=layers, temps=temps, stage=[None] * len(VECS), weights={})
-        for n in ("gsend", "gzero", "gred", "gdp", "gfin"):
+        for n in ("gsend", "gplane", "gslow"):
             simple[n] = [None] * NG
         for key, ref in zip(order, rest):
             if isinstance(key, str):
@@ -745,7 +803,7 @@
         body,
         out_shape=out_shape,
         in_specs=[any_] * (3 + n_params),
-        out_specs=[any_] * (2 + NG),
+        out_specs=[any_] * 2 + [pl.BlockSpec(memory_space=pltpu.VMEM)] * NG,
         scratch_shapes=scratch,
         compiler_params=pltpu.CompilerParams(
             collective_id=0, has_side_effects=True, vmem_limit_bytes=56 * 1024 * 1024
@@ -755,7 +813,7 @@
 
 
 def make_finish(n_dp, n_zero, params):
-    places, sizes, pieces = group_layout(n_dp, n_zero)
+    places, sizes, pieces = group_layout(n_zero)
     any_ = pl.BlockSpec(memory_space=pl.ANY)
     vmem = pl.BlockSpec(memory_space=pltpu.VMEM)
     out_shape = [jax.ShapeDtypeStruct((TOK, D), F32)] * 2
@@ -794,7 +852,6 @@
 
     def local(nodes, cotangent, lengths, *params):
         out, gx, *fins = make_fused(n_dp, n_zero, params)(lengths, nodes, cotangent, *params)
-        fins = [f.reshape(-1, D) for f in fins]
         return tuple(make_finish(n_dp, n_zero, params)(out, gx, *fins))
 
     return jax.shard_map(

time: 56.8 us -> 52.9 us (0.931)
  Pallas kernels: 55.8 us -> 51.9 us
    pallas_call x1, Pallas kernels: 53.6 us -> 49.7 us  [local(): make_fused(n_dp, n_zero, params)(lengths, nodes, cotangent, *params)]
where the time goes in v3:
time: 52.9 us; the launch traced here: 52.8 us
  Pallas kernels  51.9 us (98%)
  between operations  0.83 us (2%)
    pallas_call x1, Pallas kernels, local(): make_fused(n_dp, n_zero, params)(lengths, nodes, cotangent, *params)  49.7 us
    pallas_call x1, Pallas kernels, make_finish(): call(*[pltpu.with_memory_space_constraint(x, pltpu.VMEM) for x in xs])  2.2 us

profile of v3, /device:TPU:0, one launch (start us, length us, event | category | flops | bytes accessed | tf_op | source)
XLA Modules:
  0.0 52.8 jit_solution(14616602998200269482)
XLA Ops:
  0.7 49.7 %shard_map.322 = (f32[2048,128]{1,0:T(8,128)S(1)}, f32[2048,128]{1,0:T(8,128)S(1)}, f32[128,128]{1,0:T(8,128)S(1)}, f32[64,128]{1,0:T(8,128)S(1)}, f32[80,128]{1...) custom-call(s32[4]{0:T(128)} %refs_0_.1, ...), custom_call_target="tpu_custom_call" | custom-call | tf_op jit(solution)/shard_map/pallas_call | solution.py:854
  50.4 2.2 %shard_map.323 = (f32[2048,128]{1,0:T(8,128)}, f32[2048,128]{1,0:T(8,128)}, f32[2,32,128]{2,1,0:T(8,128)}, f32[2,32,128]{2,1,0:T(8,128)}, f32[2,32,128]{2,1,0:T(...) custom-call(f32[2048,128]{1,0:T(8,128)S(1)} %get-tuple-element.28.re, ...), custom_call_target="tpu_custom_call" | custom-call | tf_op jit(solution)/shard_map/pallas_call | solution.py:844

commit v4 on v3

--- a/solution.py
+++ b/solution.py
@@ -59,6 +59,7 @@
 )
 TMP_SCRATCH=dict(
     E=((TOK,D),F32), ED=((TOK,2*D),BF), EP=((TOK,2*FF),BF), EM=((TOK,D),F32), EO=((TOK,2*D),BF), FKV=((TOK,4*D),BF),
+    HT=((2*AUG,SEGS*D),BF), PP=((SEGS*D,2*D),BF), ES=((2,SEGS,2*D,2*D),BF),
     A2=((2*D,D),BF),
 )
 
@@ -79,10 +80,8 @@
     L['WQA'][D:,:]=pack(cat0(vec[BQ:BQ+1,:],jnp.zeros((15,D),F32)))
 
 def prep_ff(L,w):
-    up=w['up'][...]
-    L['WUP'][...]=quad(up)
-    dn=w['dn'][...]
-    L['WDN'][...]=quad(dn)
+    L['WUP'][...]=quad(w['up'][...])
+    L['WDN'][...]=quad(w['dn'][...])
 
 def prep_back(L,w):
     L['WUPT'][...]=quad_t(w['up'][...])
@@ -106,25 +105,24 @@
         y=jnp.where(lv,nn*vec[g:g+1,:]+vec[s:s+1,:],0.0)
         L[O][rows,:]=pack(y)
 
-def fwd_s(L,vec,gm,inv):
-    for s in range(SEGS):
-        rows=pl.ds(s*BLK,BLK)
-        S=jnp.where(gm,quads(tn(L['KN'][rows,:],L['VN'][rows,:]))*inv[s],0.0)
-        L['SP'][s*D:(s+1)*D,:]=pack(S)
-    T=halves(mm(L['SP'][...],L['WO2'][...]))
-    ts=[T[s*D:(s+1)*D] for s in range(SEGS)]
-    sp=[split(t) for t in ts]
-    for s in range(SEGS):
-        L['TP'][0:D,s*D:(s+1)*D]=sp[s][0]; L['TP'][D:,s*D:(s+1)*D]=sp[s][1]
-    row=cat1(*[x for hl in sp for x in hl])
-    u=mm(L['WQA'][...],cat0(row,row))
-    for s in range(SEGS):
-        us=halves(u[:,s*2*D:(s+1)*2*D])
-        L['UB'][s]=us[D:D+8]+vec[BO:BO+1,:]
-        h,l=split(us[:D])
-        p=cat1(h,l)
-        L['U2'][s,0:D,:]=p; L['U2'][s,D:,:]=p
-        L['UT2'][s,0:D,:]=cat1(h,h); L['UT2'][s,D:,:]=cat1(l,l)
+def fwd_s1(L,gm,inv,s):
+    rows=pl.ds(s*BLK,BLK)
+    S=jnp.where(gm,quads(tn(L['KN'][rows,:],L['VN'][rows,:]))*inv[s],0.0)
+    L['SP'][s*D:(s+1)*D,:]=pack(S)
+
+def fwd_s2(L,s):
+    h,l=split(halves(mm(L['SP'][s*D:(s+1)*D,:],L['WO2'][...])))
+    L['TP'][0:D,s*D:(s+1)*D]=h; L['TP'][D:,s*D:(s+1)*D]=l
+    row=cat1(h,l)
+    return cat0(row,row)
+
+def fwd_s3(L,vec,s,t2):
+    us=halves(mm(L['WQA'][...],t2))
+    L['UB'][s]=us[D:D+8]+vec[BO:BO+1,:]
+    h,l=split(us[:D])
+    p=cat1(h,l)
+    L['U2'][s,0:D,:]=p; L['U2'][s,D:,:]=p
+    L['UT2'][s,0:D,:]=cat1(h,h); L['UT2'][s,D:,:]=cat1(l,l)
 
 def fwd_c1(L,s,r0,n):
     rows=pl.ds(r0,n)
@@ -148,17 +146,11 @@
     rows=pl.ds(r0,n)
     OUT[rows,:]=mid+halves(mm(L['ACT'][rows,:],L['WDN'][...]))+vec[BD:BD+1,:]
 
-def bwd_a1(L,Tm,r0,n,fresh):
+def bwd_a1(L,Tm,r0,n):
     rows=pl.ds(r0,n)
-    if fresh:
-        e=Tm['E'][rows,:]
-        ed=pack(e); Tm['ED'][rows,:]=ed
-        se=part(e)
-    else:
-        ed=Tm['ED'][rows,:]; se=None
-    ep=halves(nt(ed,L['WDNT'][...]))*L['DG'][rows,:]
+    ep=halves(nt(Tm['ED'][rows,:],L['WDNT'][...]))*L['DG'][rows,:]
     Tm['EP'][rows,:]=pack(ep)
-    return se,part(ep)
+    return part(ep)
 
 def bwd_a2(L,Tm,r0,n):
     rows=pl.ds(r0,n)
@@ -167,39 +159,35 @@
     Tm['EO'][rows,:]=pack(em)
     return part(em)
 
-def bwd_s1(L,Tm,c):
-    hs=[]
-    for s in range(SEGS):
-        rows=pl.ds(s*BLK,BLK)
+def bwd_s1(L,Tm,s,c):
+    rows=pl.ds(s*BLK,BLK)
+    if 'XT' in L:
+        H=quads(mm(L['XT'][:,s*BLK:(s+1)*BLK],Tm['EO'][rows,:]))
+    else:
         H=quads(tn(L['X'][rows,:],Tm['EO'][rows,:]))
-        hs.append(split(cat0(H,one(c[s]),jnp.zeros((15,D),F32))))
-    return hs
-
-def bwd_s2(L,hs):
-    P=tn(L['WQA'][...],cat1(*[x for hl in hs for x in hl]))
-    P=P[:D]+P[D:]
-    pp=cat0(*[pack(halves(P[:,s*2*D:(s+1)*2*D])) for s in range(SEGS)])
-    return pp
-
-def bwd_s3(L,gm,inv,pp):
-    es=halves(nt(pp,L['WOT2'][...]))
-    out=[]
-    for s in range(SEGS):
-        e=jnp.where(gm,es[s*D:(s+1)*D]*inv[s],0.0)
-        h,l=split(e); p=cat1(h,l)
-        out.append((cat0(cat1(h,h),cat1(l,l)),cat0(p,p)))
-    return out
-
-def bwd_s4(L,hs,pp):
-    go=quads(tn(L['SP'][...],pp))
-    gq=halves(nt(cat0(cat1(*[h for h,l in hs]),cat1(*[l for h,l in hs])),L['TP'][...]))
+    h,l=split(cat0(H,one(c),jnp.zeros((15,D),F32)))
+    Tm['HT'][0:AUG,s*D:(s+1)*D]=h; Tm['HT'][AUG:,s*D:(s+1)*D]=l
+    return cat1(h,l)
+
+def bwd_s2(L,Tm,s,hp):
+    Tm['PP'][s*D:(s+1)*D,:]=pack(quads(tn(L['WQA'][...],hp)))
+
+def bwd_s3(L,Tm,gm,inv,s):
+    e=jnp.where(gm,halves(nt(Tm['PP'][s*D:(s+1)*D,:],L['WOT2'][...]))*inv[s],0.0)
+    h,l=split(e); p=cat1(h,l)
+    Tm['ES'][0,s,0:D,:]=cat1(h,h); Tm['ES'][0,s,D:,:]=cat1(l,l)
+    Tm['ES'][1,s,0:D,:]=p; Tm['ES'][1,s,D:,:]=p
+
+def bwd_s4(L,Tm):
+    go=quads(tn(L['SP'][...],Tm['PP'][...]))
+    gq=halves(nt(Tm['HT'][...],L['TP'][...]))
     gq=gq[:AUG]+gq[AUG:]
     return gq[:D],gq[D:D+1],go
 
-def bwd_b(L,vec,Tm,A2,es,r0,n,i):
+def bwd_b(L,vec,Tm,A2,s,r0,n,i):
     rows=pl.ds(r0,n)
     N,R,O,g,dot=(('NK','RK','VN',GK,nt),('NV','RV','KN',GV,mm))[i]
-    en=halves(dot(L[O][rows,:],es))
+    en=halves(dot(L[O][rows,:],Tm['ES'][i,s]))
     nn=L[N][rows,:]
     m=en*vec[g:g+1,:]
     mn=m*nn
@@ -210,7 +198,28 @@
 
 def bwd_x(L,Tm,DX,s,r0,n):
     rows=pl.ds(r0,n)
-    DX[rows,:]=Tm['EM'][rows,:]+halves(nt(Tm['FKV'][rows,:],L['WKVT'][...])+nt(Tm['EO'][rows,:],L['UT2'][s]))
+    dx=Tm['EM'][rows,:]+halves(nt(Tm['FKV'][rows,:],L['WKVT'][...])+nt(Tm['EO'][rows,:],L['UT2'][s]))
+    DX[rows,:]=dx
+    return dx
+
+def bwd_x_next(L,Tm,s,r0,n):
+    dx=bwd_x(L,Tm,Tm['E'],s,r0,n)
+    Tm['ED'][pl.ds(r0,n),:]=pack(dx)
+    return part(dx)
+
+def grad_up(L,Tm):
+    return quads(tn(L['MD'][...],Tm['EP'][...]))
+
+def grad_down(L,Tm):
+    return quads(tn(L['ACT'][...],Tm['ED'][...]))
+
+def grad_both(L,Tm):
+    g=tn(L['X'][...],Tm['FKV'][...])
+    g=g[:D]+g[D:]
+    return halves(g[:,:2*D]),halves(g[:,2*D:])
+
+def grad_one(L,Tm,i):
+    return quads(mm(L['XT'][...],Tm['FKV'][:,i*2*D:(i+1)*2*D]))
 
 
 MESH = pl.DeviceIdType.MESH
@@ -219,13 +228,13 @@
 VECS = ((4, BQ), (5, BK), (6, BV), (7, BO), (8, GK), (9, SK), (10, GV), (11, SV), (15, BD), (13, BU0))
 SMALL = 16
 GROUPS = (
-    (((1, "up"), (1, "dn")), True),
-    (((1, "q"), (1, "o")), True),
+    (((1, "up"), (1, "dn"), (1, "q"), (1, "o")), True),
     (((1, "k"), (1, "v"), (1, "small")), True),
-    (((0, "up"), (0, "dn")), True),
+    (((0, "dn"),), True),
+    (((0, "up"),), True),
     (((0, "q"), (0, "o")), True),
-    (((0, "k"),), False),
-    (((0, "small"),), True),
+    (((0, "k"),), True),
+    (((0, "small"),), False),
     (((0, "v"),), False),
 )
 PAIR = 2
@@ -266,6 +275,7 @@
     places, sizes, pieces = group_layout(n_zero)
     dp, zero = lax.axis_index("dp"), lax.axis_index("zero")
     zpeer = [None] + [lax.rem(zero + k, n_zero) for k in range(1, n_zero)]
+    zfrom = [None] + [lax.rem(zero + n_zero - k, n_zero) for k in range(1, n_zero)]
     fast, slow, n_slow = lax.rem(dp, PAIR), dp // PAIR, n_dp // PAIR
     n_plane = PAIR * n_zero
     me = fast * n_zero + zero
@@ -317,67 +327,96 @@
 
     pl.semaphore_wait(barrier, n_slow - 1 + n_plane - 1)
 
+    def place(level, name):
+        return level * 7 + (6 if name == "vec" else NAMES.index(name))
+
+    def weight_copy(level, name, k, who):
+        i = place(level, name)
+        if name == "vec":
+            src, dst = R.vec_own.at[level], R.vec_in.at[level, who]
+        else:
+            src, dst = R.params[ARG[name]].at[level], R.weights[name].at[level, rows_of(name, who), :]
+        return pltpu.make_async_remote_copy(
+            src_ref=src,
+            dst_ref=dst,
+            send_sem=R.w_send.at[i, k - 1],
+            recv_sem=R.w_recv.at[i, k - 1],
+            device_id=(dp, zpeer[k]),
+            device_id_type=MESH,
+        )
+
     n_x = n_zero // 2
     mate = zero + 1 - 2 * lax.rem(zero, 2)
     xpeer = [None] + [lax.rem(zero + 2 * k, n_zero) for k in range(1, n_x)]
     xfrom = [None] + [lax.rem(zero + n_zero - 2 * k, n_zero) for k in range(1, n_x)]
     mate_from = [None] + [lax.rem(mate + n_zero - 2 * k, n_zero) for k in range(1, n_x)]
 
-    def part_of(level, name, who):
+    def part_of(name, who):
         if name == "vec":
-            return R.vec_in.at[who]
-        return R.weights[name].at[level, rows_of(name, who), :]
-
-    def own_part(level, name):
-        return R.vec_own if name == "vec" else R.params[ARG[name]].at[level]
-
-    def place(level, name):
-        return 12 if name == "vec" else level * 6 + NAMES.index(name)
-
-    def x_copy(level, name, k, who):
-        i = place(level, name)
+            return R.vec_in.at[0, who]
+        return R.weights[name].at[0, rows_of(name, who), :]
+
+    def own_part(name):
+        return R.vec_own.at[0] if name == "vec" else R.params[ARG[name]].at[0]
+
+    def x_copy(name, k, who):
+        i = place(0, name)
         return pltpu.make_async_remote_copy(
-            src_ref=own_part(level, name),
-            dst_ref=part_of(level, name, who),
+            src_ref=own_part(name),
+            dst_ref=part_of(name, who),
             send_sem=R.x_send.at[i, k - 1],
             recv_sem=R.x_recv.at[i, k - 1],
             device_id=(dp, xpeer[k]),
             device_id_type=MESH,
         )
 
-    def mate_copy(level, name, k, who):
-        i = place(level, name)
+    def mate_copy(name, k, who):
+        i = place(0, name)
         return pltpu.make_async_remote_copy(
-            src_ref=own_part(level, name) if k == 0 else part_of(level, name, xfrom[k]),
-            dst_ref=part_of(level, name, who),
+            src_ref=own_part(name) if k == 0 else part_of(name, xfrom[k]),
+            dst_ref=part_of(name, who),
             send_sem=R.m_send.at[i, k],
             recv_sem=R.m_recv.at[i, k],
             device_id=(dp, mate),
             device_id_type=MESH,
         )
 
-    def send_weights(level, names):
+    def send_first(*names):
         for name in names:
             for k in range(1, n_x):
-                x_copy(level, name, k, zero).start()
+                x_copy(name, k, zero).start()
         for name in names:
-            mate_copy(level, name, 0, zero).start()
-
-    def relay_weights(level, names):
+            mate_copy(name, 0, zero).start()
+
+    def relay_first(*names):
         for name in names:
             for k in range(1, n_x):
-                x_copy(level, name, k, xfrom[k]).wait_recv()
-                mate_copy(level, name, k, xfrom[k]).start()
-
-    def take_weights(level, names):
+                x_copy(name, k, xfrom[k]).wait_recv()
+                mate_copy(name, k, xfrom[k]).start()
+
+    def take_first(*names):
+        for name in names:
+            if name != "vec":
+                own[0, name].wait()
+            mate_copy(name, 0, mate).wait_recv()
+            for k in range(1, n_x):
+                mate_copy(name, k, mate_from[k]).wait_recv()
+
+    far_first = sorted(range(1, n_zero), key=lambda k: k in (1, n_zero - 1))
+
+    def send_weights(level, *names):
+        for name in names:
+            for k in far_first:
+                weight_copy(level, name, k, zero).start()
+
+    def take_weights(level, *names):
         for name in names:
             if name != "vec":
                 own[level, name].wait()
-            mate_copy(level, name, 0, mate).wait_recv()
-            for k in range(1, n_x):
-                mate_copy(level, name, k, mate_from[k]).wait_recv()
-
-    send_weights(0, ("k", "v"))
+            for k in range(1, n_zero):
+                weight_copy(level, name, k, zfrom[k]).wait_recv()
+
+    send_first("k", "v", "q", "o")
 
     for c in small_in:
         c.wait()
@@ -395,7 +434,7 @@
             R.vec_own[:, row, :] = jnp.where(first, x, 0.0)
             R.vec_own[:, row + 1, :] = jnp.where(first, 0.0, x)
 
-    send_weights(0, ("vec",))
+    send_first("vec", "up", "dn")
 
     len_in.wait()
     gm = group_mask()
@@ -414,13 +453,16 @@
 
     Ls, Tm = R.layers, R.temps
     Tm["A2"] = R.A2
+    Ls[0]["XT"] = R.XT
     for y in (R.Y, R.Y2):
         y[TOK:, :] = jnp.zeros((y.shape[0] - TOK, D), F32)
     nodes_in.wait()
     for s in range(SEGS):
         x = R.nodes_v[pl.ds(st[s], BLK), :]
         Ls[0]["H"][s * BLK : (s + 1) * BLK, :] = x
-        Ls[0]["X"][s * BLK : (s + 1) * BLK, :] = pack(x)
+        x = pack(x)
+        Ls[0]["X"][s * BLK : (s + 1) * BLK, :] = x
+        R.XT[:, s * BLK : (s + 1) * BLK] = x.T
     cot_in.wait()
     sum_e = zero8 = jnp.zeros((8, D), F32)
     for s in range(SEGS):
@@ -429,45 +471,55 @@
         Tm["ED"][s * BLK : (s + 1) * BLK, :] = pack(x)
         sum_e = sum_e + part(x)
 
-    send_weights(0, ("q", "o", "up", "dn"))
-    relay_weights(0, ("k", "v", "vec"))
-    send_weights(1, NAMES)
-    take_weights(0, ("vec",))
-    vecs = []
-    for level in range(2):
+    relay_first("k", "v", "q", "o", "vec", "up", "dn")
+    send_weights(1, "k", "v", "vec", "q", "o", "up", "dn")
+    vecs = [None, None]
+
+    def take_vecs(level):
         x = R.vec_own[level]
         for k in range(1, n_zero):
-            x = x + R.vec_in[zpeer[k], level]
+            x = x + R.vec_in[level, zpeer[k]]
         R.vec[level] = x
-        vecs.append(R.vec.at[level])
+        vecs[level] = R.vec.at[level]
 
     tiles = [(s, s * BLK) for s in range(SEGS)]
 
-    def pipe(stages, hook=None):
+    def pipe(stages):
         kept = [None] * len(tiles)
         for t in range(len(tiles) + len(stages) - 1):
             for j, stage in enumerate(stages):
                 if 0 <= t - j < len(tiles):
                     kept[t - j] = stage(tiles[t - j], kept[t - j])
-            if hook is not None and t == 2:
-                hook()
         return kept
 
     for level in range(2):
-        L, vec = Ls[level], vecs[level]
+        L = Ls[level]
         dst = Ls[1]["H"] if level == 0 else R.Y
         w = {n: R.weights[n].at[level] for n in NAMES}
-        take_weights(level, ("k", "v"))
+        if level == 0:
+            take_first("k", "v", "vec")
+        else:
+            take_weights(1, "k", "v", "vec", "q", "o")
+        take_vecs(level)
+        vec = vecs[level]
         prep_kv(L, w, vec, R.A2)
+        if level == 0:
+            take_first("q", "o")
+        prep_qo(L, w, vec)
+        if level == 0:
+            take_first("up", "dn")
+            prep_ff(L, w)
         for s, r in tiles:
             fwd_a(L, vec, R.A2, live, r, BLK, level == 1)
-            if level == 0 and s == 0:
-                relay_weights(0, ("q", "o", "up", "dn"))
-        take_weights(level, ("q", "o"))
-        prep_qo(L, w, vec)
-        fwd_s(L, vec, gm, inv)
-        take_weights(level, ("up", "dn"))
-        prep_ff(L, w)
+        for s in range(SEGS):
+            fwd_s1(L, gm, inv, s)
+        t2 = [fwd_s2(L, s) for s in range(SEGS)]
+        for s in range(SEGS):
+            fwd_s3(L, vec, s, t2[s])
+        if level == 1:
+            take_weights(1, "up", "dn")
+            prep_ff(L, w)
+
         def middle(tile, _):
             return fwd_c1(L, *tile, BLK)
 
@@ -478,7 +530,7 @@
         def close(tile, mid):
             fwd_c3(L, vec, dst, mid, tile[1], BLK)
 
-        pipe([middle, hidden, close], (lambda: relay_weights(1, NAMES)) if level == 0 else None)
+        pipe([middle, hidden, close])
 
     def put(level, name, g):
         grp, at = places[level, name]
@@ -561,6 +613,20 @@
         if GROUPS[grp][1]:
             pair_copy(grp, other).wait_recv()
 
+    def hand_out_vectors():
+        small = []
+        for level in range(2):
+            g, at = places[level, "small"]
+            small.append(R.fin_out[g][at : at + SMALL, :])
+        for (_, row), out in zip(VECS, R.vec_out):
+            n = out.shape[1]
+            x = jnp.concatenate([s[row : row + 1, :] for s in small], axis=0)
+            if row == BU0:
+                x1 = jnp.concatenate([s[row + 1 : row + 2, :] for s in small], axis=0)
+                x = jnp.where(zero * n < D, x, x1)
+            x = pltpu.roll(x, lax.rem(D - lax.rem(zero * n, D), D), axis=1)
+            out[...] = x[:, :n]
+
     shift = [jnp.minimum(BLK * s - st[s], (BLK - 256) * s) for s in range(SEGS)]
 
     def unpack(Y, base):
@@ -579,51 +645,52 @@
         L, vec = Ls[level], vecs[level]
         w = {n: R.weights[n].at[level] for n in NAMES}
         prep_back(L, w)
+        put(level, "dn", grad_down(L, Tm))
+        if level == 0:
+            start_plane(2)
 
         def feed(tile, _):
-            return bwd_a1(L, Tm, tile[1], BLK, level == 0)
-
-        def after(tile, sums):
-            return (*sums, bwd_a2(L, Tm, tile[1], BLK))
+            return bwd_a1(L, Tm, tile[1], BLK)
+
+        def after(tile, su):
+            return su, bwd_a2(L, Tm, tile[1], BLK)
 
         sums = pipe([feed, after])
-        sb = sum_e if level == 1 else sum((x[0] for x in sums), zero8)
-        su = sum((x[1] for x in sums), jnp.zeros((8, FF), F32))
-        sc = [x[2] for x in sums]
-        put(level, "dn", quads(tn(L["ACT"][...], Tm["ED"][...])))
-        put(level, "up", quads(tn(L["MD"][...], Tm["EP"][...])))
-        start_plane(0 if level == 1 else 3)
+        su = sum((x[0] for x in sums), jnp.zeros((8, FF), F32))
+        sc = [x[1] for x in sums]
+        put(level, "up", grad_up(L, Tm))
         if level == 0:
+            start_plane(3)
             start_slow(0)
-        hs = bwd_s1(L, Tm, sc)
-        pp = bwd_s2(L, hs)
-        es = bwd_s3(L, gm, inv, pp)
-        gq, gbq, go = bwd_s4(L, hs, pp)
+        hp = [bwd_s1(L, Tm, s, sc[s]) for s in range(SEGS)]
+        for s in range(SEGS):
+            bwd_s2(L, Tm, s, hp[s])
+        for s in range(SEGS):
+            bwd_s3(L, Tm, gm, inv, s)
+        gq, gbq, go = bwd_s4(L, Tm)
         put(level, "q", gq)
         put(level, "o", go)
-        start_plane(1 if level == 1 else 4)
-        if level == 0:
-            start_slow(1)
+        start_plane(0 if level == 1 else 4)
         a1 = R.A2[0:D, :]
         ss = [zero8] * 6
 
         def key_value(i):
             for s, r in tiles:
-                o = bwd_b(L, vec, Tm, R.A2, es[s][i], r, BLK, i)
+                o = bwd_b(L, vec, Tm, R.A2, s, r, BLK, i)
                 for j in range(3):
                     ss[3 * i + j] = ss[3 * i + j] + o[j]
 
         key_value(0)
         if level == 0:
-            put(level, "k", center(quads(tn(L["X"][...], Tm["FKV"][:, : 2 * D])), a1))
+            put(level, "k", center(grad_one(L, Tm, 0), a1))
             start_plane(5)
-            start_slow(2)
+            start_slow(1)
         key_value(1)
         rows = [jnp.zeros((1, D), F32)] * SMALL
         rows[BQ], rows[BK], rows[BV] = gbq, one(center(ss[2], a1)), one(center(ss[5], a1))
         rows[BO] = one(sc[0] + sc[1] + sc[2] + sc[3])
         rows[SK], rows[GK], rows[SV], rows[GV] = one(ss[0]), one(ss[1]), one(ss[3]), one(ss[4])
-        rows[BD] = one(sb)
+        rows[BD] = one(sum_e)
         u = one(su)
         rows[BU0], rows[BU1] = u[:, :D], u[:, D:]
         small = jnp.concatenate(rows, axis=0)
@@ -631,44 +698,53 @@
         for p in range(n_zero):
             R.gsend[grp][p, at : at + SMALL, :] = small
         if level == 1:
-            gkv = tn(L["X"][...], Tm["FKV"][...])
-            gkv = gkv[0:D] + gkv[D:]
-            put(level, "k", center(halves(gkv[:, : 2 * D]), a1))
-            put(level, "v", center(halves(gkv[:, 2 * D :]), a1))
-            start_plane(2)
+            gk, gv = grad_both(L, Tm)
+            put(level, "k", center(gk, a1))
+            put(level, "v", center(gv, a1))
+            start_plane(1)
         else:
+            put(level, "v", center(grad_one(L, Tm, 1), a1))
+            start_plane(7)
             start_plane(6)
-            put(level, "v", center(quads(tn(L["X"][...], Tm["FKV"][:, 2 * D :])), a1))
-            start_plane(7)
-            start_slow(3)
-            start_pair(0)
-            start_pair(1)
-        dst = Tm["E"] if level == 1 else R.Y2
-        for s, r in tiles:
-            bwd_x(L, Tm, dst, s, r, BLK)
-
+            start_slow(2)
+        if level == 1:
+            sum_e = zero8
+            for s, r in tiles:
+                sum_e = sum_e + bwd_x_next(L, Tm, s, r, BLK)
+        else:
+            for s, r in tiles:
+                bwd_x(L, Tm, R.Y2, s, r, BLK)
+
+    start_slow(3)
     start_slow(4)
-    start_pair(2)
+    start_pair(0)
     unpack(R.Y, R.nodes_v)
     store_out = pltpu.make_async_copy(R.nodes_v, R.out, R.io_sem.at[3])
     store_out.start()
+    start_pair(1)
     start_slow(5)
-    start_slow(6)
     unpack(R.Y2, R.cot_v)
     store_gx = pltpu.make_async_copy(R.cot_v, R.gx, R.io_sem.at[4])
     store_gx.start()
     start_slow(7)
-    for g in (3, 4, 6, 5, 7):
+    start_slow(6)
+    for g in (2, 3, 4, 5):
         start_pair(g)
+    start_pair(6)
+    end_pair(1)
+    hand_out_vectors()
+    start_pair(7)
     for g in range(NG):
-        end_pair(g)
-
-    for level, names in ((0, NAMES + ("vec",)), (1, NAMES)):
-        for name in names:
-            mate_copy(level, name, 0, zero).wait_send()
-            for k in range(1, n_x):
-                x_copy(level, name, k, zero).wait_send()
-                mate_copy(level, name, k, xfrom[k]).wait_send()
+        if g != 1:
+            end_pair(g)
+
+    for name in NAMES + ("vec",):
+        mate_copy(name, 0, zero).wait_send()
+        for k in range(1, n_x):
+            x_copy(name, k, zero).wait_send()
+            mate_copy(name, k, xfrom[k]).wait_send()
+        for k in range(1, n_zero):
+            weight_copy(1, name, k, zero).wait_send()
     for g in range(NG):
         for k in range(1, n_plane):
             plane_copy(g, k, me).wait_send()
@@ -680,28 +756,19 @@
     store_gx.wait()
 
 
-def finish_kernel(n_dp, n_zero, order, *refs):
-    R = Names()
-    for name, ref in zip(order, refs):
-        setattr(R, name, ref)
-    places, sizes, pieces = group_layout(n_zero)
+def finish_kernel(n_zero, out, gx, fin, vec, outs, sem):
+    places, _, _ = group_layout(n_zero)
     copies = []
 
     def copy(src, dst):
-        c = pltpu.make_async_copy(src, dst, R.sem.at[len(copies)])
+        c = pltpu.make_async_copy(src, dst, sem.at[len(copies)])
         c.start()
         copies.append(c)
 
-    smalls = []
-    for level in range(2):
-        g, at = places[level, "small"]
-        c = pltpu.make_async_copy(R.fin[g].at[pl.ds(at, SMALL), :], R.small.at[level], R.small_sem.at[level])
-        c.start()
-        smalls.append(c)
     half = TOK // 2
     for i in range(2):
-        copy(R.out.at[pl.ds(i * half, half), :], R.outs[0].at[pl.ds(i * half, half), :])
-        copy(R.gx.at[pl.ds(i * half, half), :], R.outs[1].at[pl.ds(i * half, half), :])
+        copy(out.at[pl.ds(i * half, half), :], outs[0].at[pl.ds(i * half, half), :])
+        copy(gx.at[pl.ds(i * half, half), :], outs[1].at[pl.ds(i * half, half), :])
     for name, arg in ARG.items():
         for level in range(2):
             g, at = places[level, name]
@@ -709,23 +776,13 @@
             if name == "up":
                 for h in range(2):
                     copy(
-                        R.fin[g].at[pl.ds(at + h * n, n), :],
-                        R.outs[2 + arg].at[level, :, pl.ds(h * D, D)],
+                        fin[g].at[pl.ds(at + h * n, n), :],
+                        outs[2 + arg].at[level, :, pl.ds(h * D, D)],
                     )
             else:
-                copy(R.fin[g].at[pl.ds(at, n), :], R.outs[2 + arg].at[level])
-    zero = lax.axis_index("zero")
-    for c in smalls:
-        c.wait()
-    small = [R.small[level] for level in range(2)]
-    for arg, row in VECS:
-        n = R.outs[2 + arg].shape[1]
-        x = jnp.concatenate([s[row : row + 1, :] for s in small], axis=0)
-        if row == BU0:
-            x1 = jnp.concatenate([s[row + 1 : row + 2, :] for s in small], axis=0)
-            x = jnp.where(zero * n < D, x, x1)
-        x = pltpu.roll(x, lax.rem(D - lax.rem(zero * n, D), D), axis=1)
-        R.outs[2 + arg][...] = x[:, :n]
+                copy(fin[g].at[pl.ds(at, n), :], outs[2 + arg].at[level])
+    for (arg, _), v in zip(VECS, vec):
+        copy(v, outs[2 + arg])
     for c in copies:
         c.wait()
 
@@ -742,6 +799,7 @@
 
     n_params = len(params)
     out_shape = [VM((TOK, D), F32)] * 2 + [VM((p, D), F32) for p in sizes]
+    out_shape += [VM(params[arg].shape, F32) for arg, _ in VECS]
     ls, ts = list(LAYER_SCRATCH), [n for n in TMP_SCRATCH if n != "A2"]
     for level in range(2):
         for n in ls:
@@ -751,6 +809,7 @@
     add("lengths", pltpu.SMEM((SEGS,), jnp.int32))
     add("A2", VM(*TMP_SCRATCH["A2"]))
     add("Y", VM((TOK + 768, D), F32))
+    add("XT", VM((2 * D, TOK), BF))
     add("Y2", VM((TOK + 768, D), F32))
     add("nodes_v", VM((TOK, D), F32))
     add("cot_v", VM((TOK, D), F32))
@@ -760,7 +819,7 @@
         rows, cols = shard(n, n_zero)
         add(("weights", n), VM((2, rows * n_zero, cols), F32))
     add("vec_own", VM((2, SMALL, D), F32))
-    add("vec_in", VM((n_zero, 2, SMALL, D), F32))
+    add("vec_in", VM((2, n_zero, SMALL, D), F32))
     add("vec", VM((2, SMALL, D), F32))
     for g in range(NG):
         add(("gsend", g), VM((n_zero, sizes[g], D), F32))
@@ -769,9 +828,11 @@
     add("stage_sem", dma((len(VECS),)))
     add("io_sem", dma((5,)))
     add("own_sem", dma((2, 6)))
+    add("w_send", dma((14, n_zero - 1)))
+    add("w_recv", dma((14, n_zero - 1)))
     for n, m in (("x", n_zero // 2 - 1), ("m", n_zero // 2)):
-        add(n + "_send", dma((13, m)))
-        add(n + "_recv", dma((13, m)))
+        add(n + "_send", dma((7, m)))
+        add(n + "_recv", dma((7, m)))
     for n, m in (("p", PAIR * n_zero), ("s", n_dp // PAIR)):
         add(n + "_send", dma((NG, m - 1)))
         add(n + "_recv", dma((NG, m - 1)))
@@ -781,9 +842,10 @@
     def body(*refs):
         lengths_in, nodes, cot = refs[:3]
         pr = refs[3 : 3 + n_params]
-        outs = refs[3 + n_params : 5 + NG + n_params]
-        rest = refs[5 + NG + n_params :]
-        simple = dict(lengths_in=lengths_in, nodes=nodes, cotangent=cot, params=pr, out=outs[0], gx=outs[1], fin_out=outs[2:])
+        n_outs = 2 + NG + len(VECS)
+        outs = refs[3 + n_params : 3 + n_outs + n_params]
+        rest = refs[3 + n_outs + n_params :]
+        simple = dict(lengths_in=lengths_in, nodes=nodes, cotangent=cot, params=pr, out=outs[0], gx=outs[1], fin_out=outs[2 : 2 + NG], vec_out=outs[2 + NG :])
         layers, temps = [{}, {}], {}
         simple.update(layers=layers, temps=temps, stage=[None] * len(VECS), weights={})
         for n in ("gsend", "gplane", "gslow"):
@@ -803,7 +865,7 @@
         body,
         out_shape=out_shape,
         in_specs=[any_] * (3 + n_params),
-        out_specs=[any_] * 2 + [pl.BlockSpec(memory_space=pltpu.VMEM)] * NG,
+        out_specs=[any_] * 2 + [pl.BlockSpec(memory_space=pltpu.VMEM)] * (NG + len(VECS)),
         scratch_shapes=scratch,
         compiler_params=pltpu.CompilerParams(
             collective_id=0, has_side_effects=True, vmem_limit_bytes=56 * 1024 * 1024
@@ -812,34 +874,23 @@
     return call
 
 
-def make_finish(n_dp, n_zero, params):
-    places, sizes, pieces = group_layout(n_zero)
+def make_finish(n_zero, params):
     any_ = pl.BlockSpec(memory_space=pl.ANY)
-    vmem = pl.BlockSpec(memory_space=pltpu.VMEM)
     out_shape = [jax.ShapeDtypeStruct((TOK, D), F32)] * 2
     out_shape += [jax.ShapeDtypeStruct(p.shape, F32) for p in params]
-    weights = set(ARG.values())
-    out_specs = [any_] * 2 + [any_ if i in weights else vmem for i in range(len(params))]
+    n_ins = 2 + NG + len(VECS)
 
     def body(*refs):
         out, gx = refs[:2]
-        fin = refs[2 : 2 + NG]
-        outs = refs[2 + NG : 4 + NG + len(params)]
-        rest = refs[4 + NG + len(params) :]
-        simple = dict(out=out, gx=gx, fin=fin, outs=outs, small=rest[0], sem=rest[1], small_sem=rest[2])
-        finish_kernel(n_dp, n_zero, list(simple), *simple.values())
+        fin, vec = refs[2 : 2 + NG], refs[2 + NG : n_ins]
+        finish_kernel(n_zero, out, gx, fin, vec, refs[n_ins:-1], refs[-1])
 
     call = pl.pallas_call(
         body,
         out_shape=out_shape,
-        in_specs=[any_] * (2 + NG),
-        out_specs=out_specs,
-        scratch_shapes=[
-            VM((2, SMALL, D), F32),
-            pltpu.SemaphoreType.DMA((18,)),
-            pltpu.SemaphoreType.DMA((2,)),
-        ],
-        compiler_params=pltpu.CompilerParams(vmem_limit_bytes=16 * 1024 * 1024),
+        in_specs=[any_] * n_ins,
+        out_specs=[any_] * len(out_shape),
+        scratch_shapes=[pltpu.SemaphoreType.DMA((28,))],
     )
     return lambda *xs: call(*[pltpu.with_memory_space_constraint(x, pltpu.VMEM) for x in xs])
 
@@ -851,8 +902,8 @@
     rows = P(("dp", "zero"), None)
 
     def local(nodes, cotangent, lengths, *params):
-        out, gx, *fins = make_fused(n_dp, n_zero, params)(lengths, nodes, cotangent, *params)
-        return tuple(make_finish(n_dp, n_zero, params)(out, gx, *fins))
+        results = make_fused(n_dp, n_zero, params)(lengths, nodes, cotangent, *params)
+        return tuple(make_finish(n_zero, params)(*results))
 
     return jax.shard_map(
         local,

time: 52.9 us -> 51.7 us (0.977); the launches traced: 52.8 us -> 50.8 us
  Pallas kernels: 51.9 us -> 49.9 us
    pallas_call x1, Pallas kernels: 49.7 us -> 48.3 us  [local(): make_fused(n_dp, n_zero, params)(lengths, nodes, cotangent, *params)]
    pallas_call x1, Pallas kernels: 2.2 us -> 1.67 us  [make_finish(): call(*[pltpu.with_memory_space_constraint(x, pltpu.VMEM) for x in xs])]
where the time goes in v4:
time: 51.7 us; the launch traced here: 50.8 us
  Pallas kernels  49.9 us (97%)
  between operations  0.83 us (2%)
    pallas_call x1, Pallas kernels, local(): make_fused(n_dp, n_zero, params)(lengths, nodes, cotangent, *params)  48.3 us
    pallas_call x1, Pallas kernels, make_finish(): call(*[pltpu.with_memory_space_constraint(x, pltpu.VMEM) for x in xs])  1.67 us

profile of v4, /device:TPU:0, one launch (start us, length us, event | category | flops | bytes accessed | tf_op | source)
XLA Modules:
  0.0 50.8 jit_solution(1607817543296014743)
XLA Ops:
  0.7 48.3 %shard_map.322 = (f32[2048,128]{1,0:T(8,128)S(1)}, f32[2048,128]{1,0:T(8,128)S(1)}, f32[192,128]{1,0:T(8,128)S(1)}, f32[80,128]{1,0:T(8,128)S(1)}, f32[64,128]{1...) custom-call(s32[4]{0:T(128)} %refs_0_.1, ...), custom_call_target="tpu_custom_call" | custom-call | tf_op jit(solution)/shard_map/pallas_call | solution.py:905
  48.9 1.7 %shard_map.323 = (f32[2048,128]{1,0:T(8,128)}, f32[2048,128]{1,0:T(8,128)}, f32[2,32,128]{2,1,0:T(8,128)}, f32[2,32,128]{2,1,0:T(8,128)}, f32[2,32,128]{2,1,0:T(...) custom-call(f32[2048,128]{1,0:T(8,128)S(1)} %get-tuple-element.38.re, ...), custom_call_target="tpu_custom_call" | custom-call | tf_op jit(solution)/shard_map/pallas_call | solution.py:895

commit v5 on v4

--- a/solution.py
+++ b/solution.py
@@ -230,12 +230,9 @@
 GROUPS = (
     (((1, "up"), (1, "dn"), (1, "q"), (1, "o")), True),
     (((1, "k"), (1, "v"), (1, "small")), True),
-    (((0, "dn"),), True),
-    (((0, "up"),), True),
+    (((0, "dn"), (0, "up")), True),
     (((0, "q"), (0, "o")), True),
-    (((0, "k"),), True),
-    (((0, "small"),), False),
-    (((0, "v"),), False),
+    (((0, "k"), (0, "v"), (0, "small")), 2),
 )
 PAIR = 2
 NG = len(GROUPS)
@@ -293,7 +290,8 @@
 
     barrier = pltpu.get_barrier_semaphore()
     for k in range(1, n_slow):
-        pl.semaphore_signal(barrier, inc=1, device_id=along(k), device_id_type=MESH)
+        for f in range(PAIR):
+            pl.semaphore_signal(barrier, inc=1, device_id=(speer[k] * PAIR + f, zero), device_id_type=MESH)
     for k in range(1, n_plane):
         pl.semaphore_signal(barrier, inc=1, device_id=in_plane(k), device_id_type=MESH)
 
@@ -325,7 +323,7 @@
     cot_in = pltpu.make_async_copy(R.cotangent, R.cot_v, R.io_sem.at[1])
     cot_in.start()
 
-    pl.semaphore_wait(barrier, n_slow - 1 + n_plane - 1)
+    pl.semaphore_wait(barrier, PAIR * (n_slow - 1) + n_plane - 1)
 
     def place(level, name):
         return level * 7 + (6 if name == "vec" else NAMES.index(name))
@@ -434,7 +432,7 @@
             R.vec_own[:, row, :] = jnp.where(first, x, 0.0)
             R.vec_own[:, row + 1, :] = jnp.where(first, 0.0, x)
 
-    send_first("vec", "up", "dn")
+    send_first("vec")
 
     len_in.wait()
     gm = group_mask()
@@ -471,8 +469,9 @@
         Tm["ED"][s * BLK : (s + 1) * BLK, :] = pack(x)
         sum_e = sum_e + part(x)
 
-    relay_first("k", "v", "q", "o", "vec", "up", "dn")
-    send_weights(1, "k", "v", "vec", "q", "o", "up", "dn")
+    send_weights(0, "up", "dn")
+    relay_first("k", "v", "vec", "q", "o")
+    send_weights(1, "k", "v", "vec", "q", "o")
     vecs = [None, None]
 
     def take_vecs(level):
@@ -494,7 +493,6 @@
 
     for level in range(2):
         L = Ls[level]
-        dst = Ls[1]["H"] if level == 0 else R.Y
         w = {n: R.weights[n].at[level] for n in NAMES}
         if level == 0:
             take_first("k", "v", "vec")
@@ -506,9 +504,6 @@
         if level == 0:
             take_first("q", "o")
         prep_qo(L, w, vec)
-        if level == 0:
-            take_first("up", "dn")
-            prep_ff(L, w)
         for s, r in tiles:
             fwd_a(L, vec, R.A2, live, r, BLK, level == 1)
         for s in range(SEGS):
@@ -516,9 +511,10 @@
         t2 = [fwd_s2(L, s) for s in range(SEGS)]
         for s in range(SEGS):
             fwd_s3(L, vec, s, t2[s])
-        if level == 1:
-            take_weights(1, "up", "dn")
-            prep_ff(L, w)
+        take_weights(level, "up", "dn")
+        if level == 0:
+            send_weights(1, "up", "dn")
+        prep_ff(L, w)
 
         def middle(tile, _):
             return fwd_c1(L, *tile, BLK)
@@ -528,7 +524,10 @@
             return mid
 
         def close(tile, mid):
-            fwd_c3(L, vec, dst, mid, tile[1], BLK)
+            if level == 0:
+                fwd_c3(L, vec, Ls[1]["H"], mid, tile[1], BLK)
+            else:
+                R.Y[pl.ds(tile[1], BLK), :] = mid
 
         pipe([middle, hidden, close])
 
@@ -566,6 +565,19 @@
             device_id_type=MESH,
         )
 
+    dpeer = [None] + [lax.rem(dp + k, n_dp) for k in range(1, n_dp)]
+    dfrom = [None] + [lax.rem(dp + n_dp - k, n_dp) for k in range(1, n_dp)]
+
+    def dp_copy(grp, k, who):
+        return pltpu.make_async_remote_copy(
+            src_ref=R.gslow[grp].at[dp],
+            dst_ref=R.gslow[grp].at[who],
+            send_sem=R.s_send.at[grp, k - 1],
+            recv_sem=R.s_recv.at[grp, k - 1],
+            device_id=(dpeer[k], zero),
+            device_id_type=MESH,
+        )
+
     def half_of(grp, who):
         rows = pieces[grp]
         return R.fin_out[grp].at[pl.ds(pl.multiple_of(who * rows, 8), rows), :]
@@ -593,11 +605,26 @@
         x = R.gplane[grp][0]
         for j in range(1, n_plane):
             x = x + R.gplane[grp][j]
-        R.gslow[grp][slow] = x
-        for k in range(1, n_slow):
-            slow_copy(grp, k, slow).start()
+        if GROUPS[grp][1] == 2:
+            R.gslow[grp][dp] = x
+            for k in range(1, n_dp):
+                dp_copy(grp, k, dp).start()
+        else:
+            R.gslow[grp][slow] = x
+            for k in range(1, n_slow):
+                slow_copy(grp, k, slow).start()
 
     def start_pair(grp):
+        if GROUPS[grp][1] == 2:
+            for k in range(1, n_dp):
+                dp_copy(grp, k, dfrom[k]).wait_recv()
+            rows = pieces[grp]
+            for f in range(PAIR):
+                x = R.gslow[grp][f]
+                for j in range(1, n_slow):
+                    x = x + R.gslow[grp][j * PAIR + f]
+                R.fin_out[grp][f * rows : (f + 1) * rows, :] = x
+            return
         for k in range(1, n_slow):
             slow_copy(grp, k, sfrom[k]).wait_recv()
         x = R.gslow[grp][0]
@@ -610,7 +637,7 @@
             R.fin_out[grp][...] = x
 
     def end_pair(grp):
-        if GROUPS[grp][1]:
+        if GROUPS[grp][1] == 1:
             pair_copy(grp, other).wait_recv()
 
     def hand_out_vectors():
@@ -646,8 +673,6 @@
         w = {n: R.weights[n].at[level] for n in NAMES}
         prep_back(L, w)
         put(level, "dn", grad_down(L, Tm))
-        if level == 0:
-            start_plane(2)
 
         def feed(tile, _):
             return bwd_a1(L, Tm, tile[1], BLK)
@@ -660,17 +685,17 @@
         sc = [x[1] for x in sums]
         put(level, "up", grad_up(L, Tm))
         if level == 0:
-            start_plane(3)
+            start_plane(2)
             start_slow(0)
         hp = [bwd_s1(L, Tm, s, sc[s]) for s in range(SEGS)]
         for s in range(SEGS):
             bwd_s2(L, Tm, s, hp[s])
-        for s in range(SEGS):
-            bwd_s3(L, Tm, gm, inv, s)
         gq, gbq, go = bwd_s4(L, Tm)
         put(level, "q", gq)
         put(level, "o", go)
-        start_plane(0 if level == 1 else 4)
+        for s in range(SEGS):
+            bwd_s3(L, Tm, gm, inv, s)
+        start_plane(0 if level == 1 else 3)
         a1 = R.A2[0:D, :]
         ss = [zero8] * 6
 
@@ -681,10 +706,6 @@
                     ss[3 * i + j] = ss[3 * i + j] + o[j]
 
         key_value(0)
-        if level == 0:
-            put(level, "k", center(grad_one(L, Tm, 0), a1))
-            start_plane(5)
-            start_slow(1)
         key_value(1)
         rows = [jnp.zeros((1, D), F32)] * SMALL
         rows[BQ], rows[BK], rows[BV] = gbq, one(center(ss[2], a1)), one(center(ss[5], a1))
@@ -703,10 +724,10 @@
             put(level, "v", center(gv, a1))
             start_plane(1)
         else:
+            put(level, "k", center(grad_one(L, Tm, 0), a1))
             put(level, "v", center(grad_one(L, Tm, 1), a1))
-            start_plane(7)
-            start_plane(6)
-            start_slow(2)
+            start_plane(4)
+            start_slow(1)
         if level == 1:
             sum_e = zero8
             for s, r in tiles:
@@ -715,39 +736,46 @@
             for s, r in tiles:
                 bwd_x(L, Tm, R.Y2, s, r, BLK)
 
+    start_slow(2)
     start_slow(3)
-    start_slow(4)
     start_pair(0)
+    start_pair(1)
+    for s, r in tiles:
+        fwd_c3(Ls[1], vecs[1], R.Y, R.Y[pl.ds(r, BLK), :], r, BLK)
     unpack(R.Y, R.nodes_v)
     store_out = pltpu.make_async_copy(R.nodes_v, R.out, R.io_sem.at[3])
     store_out.start()
-    start_pair(1)
-    start_slow(5)
+    start_slow(4)
+    start_pair(2)
+    start_pair(3)
     unpack(R.Y2, R.cot_v)
     store_gx = pltpu.make_async_copy(R.cot_v, R.gx, R.io_sem.at[4])
     store_gx.start()
-    start_slow(7)
-    start_slow(6)
-    for g in (2, 3, 4, 5):
-        start_pair(g)
-    start_pair(6)
+    start_pair(4)
+    end_pair(0)
     end_pair(1)
+    end_pair(2)
+    end_pair(3)
+    end_pair(4)
     hand_out_vectors()
-    start_pair(7)
-    for g in range(NG):
-        if g != 1:
-            end_pair(g)
-
     for name in NAMES + ("vec",):
-        mate_copy(name, 0, zero).wait_send()
-        for k in range(1, n_x):
-            x_copy(name, k, zero).wait_send()
-            mate_copy(name, k, xfrom[k]).wait_send()
+        if name in ("up", "dn"):
+            for k in range(1, n_zero):
+                weight_copy(0, name, k, zero).wait_send()
+        else:
+            mate_copy(name, 0, zero).wait_send()
+            for k in range(1, n_x):
+                x_copy(name, k, zero).wait_send()
+                mate_copy(name, k, xfrom[k]).wait_send()
         for k in range(1, n_zero):
             weight_copy(1, name, k, zero).wait_send()
     for g in range(NG):
         for k in range(1, n_plane):
             plane_copy(g, k, me).wait_send()
+        if GROUPS[g][1] == 2:
+            for k in range(1, n_dp):
+                dp_copy(g, k, dp).wait_send()
+            continue
         for k in range(1, n_slow):
             slow_copy(g, k, slow).wait_send()
         if GROUPS[g][1]:
@@ -824,7 +852,7 @@
     for g in range(NG):
         add(("gsend", g), VM((n_zero, sizes[g], D), F32))
         add(("gplane", g), VM((PAIR * n_zero, pieces[g], D), F32))
-        add(("gslow", g), VM((n_dp // PAIR, pieces[g], D), F32))
+        add(("gslow", g), VM((n_dp, pieces[g], D), F32))
     add("stage_sem", dma((len(VECS),)))
     add("io_sem", dma((5,)))
     add("own_sem", dma((2, 6)))
@@ -833,7 +861,7 @@
     for n, m in (("x", n_zero // 2 - 1), ("m", n_zero // 2)):
         add(n + "_send", dma((7, m)))
         add(n + "_recv", dma((7, m)))
-    for n, m in (("p", PAIR * n_zero), ("s", n_dp // PAIR)):
+    for n, m in (("p", PAIR * n_zero), ("s", n_dp)):
         add(n + "_send", dma((NG, m - 1)))
         add(n + "_recv", dma((NG, m - 1)))
     add("f_send", dma((NG,)))

time: 51.7 us -> 49.5 us (0.957); the launches traced: 50.8 us -> 49.3 us
  Pallas kernels: 49.9 us -> 48.5 us
    pallas_call x1, Pallas kernels: 48.3 us -> 46.8 us  [local(): make_fused(n_dp, n_zero, params)(lengths, nodes, cotangent, *params)]
where the time goes in v5:
time: 49.5 us; the launch traced here: 49.3 us
  Pallas kernels  48.5 us (98%)
  between operations  0.83 us (2%)
    pallas_call x1, Pallas kernels, local(): make_fused(n_dp, n_zero, params)(lengths, nodes, cotangent, *params)  46.8 us
    pallas_call x1, Pallas kernels, make_finish(): call(*[pltpu.with_memory_space_constraint(x, pltpu.VMEM) for x in xs])  1.67 us

profile of v5, /device:TPU:0, one launch (start us, length us, event | category | flops | bytes accessed | tf_op | source)
XLA Modules:
  0.0 49.3 jit_solution(14848443260454074688)
XLA Ops:
  0.7 46.8 %shard_map.322 = (f32[2048,128]{1,0:T(8,128)S(1)}, f32[2048,128]{1,0:T(8,128)S(1)}, f32[192,128]{1,0:T(8,128)S(1)}, f32[80,128]{1,0:T(8,128)S(1)}, f32[128,128]{...) custom-call(s32[4]{0:T(128)} %refs_0_.1, ...), custom_call_target="tpu_custom_call" | custom-call | tf_op jit(solution)/shard_map/pallas_call | solution.py:933
  47.5 1.7 %shard_map.323 = (f32[2048,128]{1,0:T(8,128)}, f32[2048,128]{1,0:T(8,128)}, f32[2,32,128]{2,1,0:T(8,128)}, f32[2,32,128]{2,1,0:T(8,128)}, f32[2,32,128]{2,1,0:T(...) custom-call(f32[2048,128]{1,0:T(8,128)S(1)} %get-tuple-element.35.re, ...), custom_call_target="tpu_custom_call" | custom-call | tf_op jit(solution)/shard_map/pallas_call | solution.py:923

commit v6 on v5

--- a/solution.py
+++ b/solution.py
@@ -214,7 +214,7 @@
     return quads(tn(L['ACT'][...],Tm['ED'][...]))
 
 def grad_both(L,Tm):
-    g=tn(L['X'][...],Tm['FKV'][...])
+    g=mm(L['XT'][...],Tm['FKV'][...]) if 'XT' in L else tn(L['X'][...],Tm['FKV'][...])
     g=g[:D]+g[D:]
     return halves(g[:,:2*D]),halves(g[:,2*D:])
 
@@ -470,8 +470,10 @@
         sum_e = sum_e + part(x)
 
     send_weights(0, "up", "dn")
-    relay_first("k", "v", "vec", "q", "o")
-    send_weights(1, "k", "v", "vec", "q", "o")
+    relay_first("k", "v")
+    send_weights(1, "k", "v", "vec")
+    relay_first("vec", "q", "o")
+    send_weights(1, "q", "o")
     vecs = [None, None]
 
     def take_vecs(level):
@@ -672,7 +674,6 @@
         L, vec = Ls[level], vecs[level]
         w = {n: R.weights[n].at[level] for n in NAMES}
         prep_back(L, w)
-        put(level, "dn", grad_down(L, Tm))
 
         def feed(tile, _):
             return bwd_a1(L, Tm, tile[1], BLK)
@@ -683,6 +684,7 @@
         sums = pipe([feed, after])
         su = sum((x[0] for x in sums), jnp.zeros((8, FF), F32))
         sc = [x[1] for x in sums]
+        put(level, "dn", grad_down(L, Tm))
         put(level, "up", grad_up(L, Tm))
         if level == 0:
             start_plane(2)
@@ -724,8 +726,9 @@
             put(level, "v", center(gv, a1))
             start_plane(1)
         else:
-            put(level, "k", center(grad_one(L, Tm, 0), a1))
-            put(level, "v", center(grad_one(L, Tm, 1), a1))
+            gk, gv = grad_both(L, Tm)
+            put(level, "k", center(gk, a1))
+            put(level, "v", center(gv, a1))
             start_plane(4)
             start_slow(1)
         if level == 1:

time: 49.5 us -> 50.1 us (1.012); the launches traced: 49.3 us -> 49.4 us
  no operation moved by 1% of the time
where the time goes in v6:
time: 50.1 us; the launch traced here: 49.4 us
  Pallas kernels  48.6 us (97%)
  between operations  0.83 us (2%)
    pallas_call x1, Pallas kernels, local(): make_fused(n_dp, n_zero, params)(lengths, nodes, cotangent, *params)  46.9 us
    pallas_call x1, Pallas kernels, make_finish(): call(*[pltpu.with_memory_space_constraint(x, pltpu.VMEM) for x in xs])  1.67 us

profile of v6, /device:TPU:0, one launch (start us, length us, event | category | flops | bytes accessed | tf_op | source)
XLA Modules:
  0.0 49.4 jit_solution(1366581296501294160)
XLA Ops:
  0.7 46.9 %shard_map.322 = (f32[2048,128]{1,0:T(8,128)S(1)}, f32[2048,128]{1,0:T(8,128)S(1)}, f32[192,128]{1,0:T(8,128)S(1)}, f32[80,128]{1,0:T(8,128)S(1)}, f32[128,128]{...) custom-call(s32[4]{0:T(128)} %refs_0_.1, ...), custom_call_target="tpu_custom_call" | custom-call | tf_op jit(solution)/shard_map/pallas_call | solution.py:936
  47.6 1.7 %shard_map.323 = (f32[2048,128]{1,0:T(8,128)}, f32[2048,128]{1,0:T(8,128)}, f32[2,32,128]{2,1,0:T(8,128)}, f32[2,32,128]{2,1,0:T(8,128)}, f32[2,32,128]{2,1,0:T(...) custom-call(f32[2048,128]{1,0:T(8,128)S(1)} %get-tuple-element.35.re, ...), custom_call_target="tpu_custom_call" | custom-call | tf_op jit(solution)/shard_map/pallas_call | solution.py:926
